TPU v7x, 32 devices: a whole 2x2x4 slice. The times are simulated.
32 devices in a mesh: section: 4 (over y, x), dp: 8 (over z, core).
Axes of the slice: x: 2, y: 2, z: 4, core: 2. Of those that a mesh axis runs over, the one named last changes fastest.
Arguments:
- states_in: bfloat16 [16, 1024, 512], P('dp', None, 'section'), may hold values from -6 to 6
- memory: bfloat16 [16, 1024, 512], P('dp', None, 'section'), may hold values from -6 to 6
- cotangent: bfloat16 [16, 1024, 512], P('dp', None, 'section'), may hold values from -6 to 6
- weight_bank: bfloat16 [4, 8, 512, 512], P('section')
- gain_bank: float32 [4, 2, 512], P('section'), may hold values from 0.1 to 1.9
- segments: int32 [16, 1024], P('dp'), may hold values from 0 to 7, as said below
- pad_mask: int32 [16, 1024], P('dp'), may hold values from 0 to 1, as said below
- memory_segments: int32 [16, 1024], P('dp'), may hold values from 0 to 7, as said below
- memory_mask: int32 [16, 1024], P('dp'), may hold values from 0 to 1, as said below
- exit_depths: int32 [16, 8], P('dp'), may hold values from 1 to 2
Outputs:
- states: bfloat16 [16, 1024, 512], P('dp', None, 'section')
- halting: float32 [16, 2, 1024], P('dp', None, 'section')
- input_grad: float32 [16, 1024, 512], P('dp', None, 'section')
- memory_grad: float32 [16, 1024, 512], P('dp', None, 'section')
- bank_grad: float32 [4, 8, 512, 512], P('section')
- gain_grad: float32 [4, 2, 512], P('section')
Inputs may be any that keep to these rules, and one draw needn't show every extreme that they name: `segments`: each row holds 8 sentences numbered in order from 0, each at least two filled slots long; the padding slots after a row's filled slots carry the number 8 - 1. `pad_mask`: a row's filled slots come first, its padding after them. `memory_segments`: each row's memory holds 8 source sentences numbered in order from 0, each at least two filled slots long; padding slots after them carry the number 8 - 1. `memory_mask`: a row's filled memory slots come first, its padding after them. `exit_depths`: a sentence of depth 1 leaves after the first layer, of depth 2 after the second.
All inputs are finite; a program needn't handle non-finite values.
Results may differ from a plain program's by a relative error of at most 0.025.
Values may be sent and summed in bfloat16 or wider, within the bound.
A program may use at most 256 MiB of HBM per device.

v0:
```python
import functools

import jax
import jax.numpy as jnp
from jax import lax
from jax.experimental import pallas as pl
from jax.experimental.pallas import tpu as pltpu
from jax.sharding import PartitionSpec as P

HEADS = 8
EPS = 1e-06
BLOCK = 128
KEYS = 256
STEP = 16
NEG = -1e30

bf16 = jnp.bfloat16
f32 = jnp.float32
i32 = jnp.int32

SELF, CROSS = 0, 2
CORE, FLAG_T, FIRST, LAST, TOP_T = 8, 9, 10, 11, 12
FLAG_M, TOP_M = 13, 14


def dot(left, right):
    return jnp.dot(left, right, preferred_element_type=f32)


def dot_nt(left, right):
    return lax.dot_general(left, right, (((1,), (1,)), ((), ())), preferred_element_type=f32)


def dot_tn(left, right):
    return lax.dot_general(left, right, (((0,), (0,)), ((), ())), preferred_element_type=f32)


def exact_nt(left, right):
    return lax.dot_general(
        left, right, (((1,), (1,)), ((), ())), precision=lax.Precision.HIGHEST, preferred_element_type=f32
    )


def exact(left, right):
    return jnp.dot(left, right, precision=lax.Precision.HIGHEST, preferred_element_type=f32)


def norm(x, gain):
    return x * lax.rsqrt(jnp.mean(x * x, axis=-1, keepdims=True) + EPS) * gain


def norm_back(x, gain, grad):
    rate = lax.rsqrt(jnp.mean(x * x, axis=-1, keepdims=True) + EPS)
    scaled = x * rate
    inner = grad * gain
    grad_x = rate * (inner - scaled * jnp.mean(inner * scaled, axis=-1, keepdims=True))
    return grad_x, jnp.sum(grad * scaled, axis=0, keepdims=True)


GELU_A = 0.7978845608028654
GELU_B = 0.044715


def gelu(z):
    return 0.5 * z * (1.0 + jnp.tanh(GELU_A * (z + GELU_B * z * z * z)))


def gelu_both(z):
    square = z * z
    bend = jnp.tanh(GELU_A * z * (1.0 + GELU_B * square))
    half = 0.5 * (1.0 + bend)
    slope = half + 0.5 * z * (1.0 - bend * bend) * (GELU_A * (1.0 + 3.0 * GELU_B * square))
    return z * half, slope


def windows(meta, length):
    wide = length * 5 // 8
    slim = length - wide
    core = meta[0, CORE]
    return (
        pl.ds(pl.multiple_of(core * slim, BLOCK), wide),
        pl.ds(pl.multiple_of((1 - core) * wide, BLOCK), slim),
    )


def over(meta, flag, length, work):
    main, other = windows(meta, length)
    work(main, True)

    @pl.when(meta[0, flag] == 1)
    def _():
        work(other, False)


class Moves:
    def __init__(self, meta, length, semaphores):
        self.meta, self.semaphores, self.used, self.leaving = meta, semaphores, 0, []
        self.rows = windows(meta, length)

    def copy(self, src, dst):
        self.used += 1
        return pltpu.make_async_copy(src, dst, self.semaphores.at[self.used - 1])

    def whole(self, src, dst):
        copy = self.copy(src, dst)
        copy.start()
        return copy.wait

    def pair(self, src, dst, flag):
        first, second = (self.copy(src.at[rows], dst.at[rows]) for rows in self.rows)
        first.start()
        pl.when(self.meta[0, flag] == 1)(second.start)

        def wait():
            first.wait()
            pl.when(self.meta[0, flag] == 1)(second.wait)

        return wait

    def away(self, src, dst, flag=None):
        self.leaving.append(self.whole(src, dst) if flag is None else self.pair(src, dst, flag))

    def finish(self):
        for wait in self.leaving:
            wait()


def block(i):
    return pl.ds(pl.multiple_of(i * BLOCK, BLOCK), BLOCK)


def lanes_of(at, p):
    return slice(at + p * BLOCK, at + (p + 1) * BLOCK)


def two_heads(tile, lane):
    zero = jnp.zeros_like(tile)
    return jnp.concatenate([jnp.where(lane < 64, tile, zero), jnp.where(lane < 64, zero, tile)], axis=0)


def both_blocks(tile):
    return jnp.concatenate([tile[:64, :BLOCK], tile[64:, BLOCK:]], axis=0)


def key_window(meta, kind, top, i, n, low, high):
    wanted = meta[i, kind] + n * KEYS
    start = pl.multiple_of(jnp.minimum(wanted, meta[0, top]), STEP)
    place = lax.broadcasted_iota(i32, (KEYS, BLOCK), 0) + start
    bias = jnp.where((place >= jnp.maximum(low, wanted)) & (place < high), 0.0, NEG)
    return pl.ds(start, KEYS), jnp.concatenate([bias, bias], axis=1)


def two_rows(rows_ref, p, rows):
    return jnp.concatenate([rows_ref[2 * p : 2 * p + 1, rows], rows_ref[2 * p + 1 : 2 * p + 2, rows]], axis=1)


def attend(meta, kind, top, info, info_row, q, k, v, o, lse, both_q, peaks, totals, sums):
    (q, q_at), (k, k_at), (v, v_at) = q, k, v
    pairs = o.shape[1] // BLOCK

    def one_block(i, _):
        count = (meta[i, kind + 1] - meta[i, kind] + KEYS - 1) // KEYS

        @pl.when(count > 0)
        def _():
            rows = block(i)
            lane = lax.broadcasted_iota(i32, (BLOCK, BLOCK), 1)
            low, high = info[info_row : info_row + 1, rows], info[info_row + 1 : info_row + 2, rows]
            peaks[...] = jnp.full(peaks.shape, -jnp.inf, f32)
            totals[...] = jnp.zeros(totals.shape, f32)
            sums[...] = jnp.zeros(sums.shape, f32)
            for p in range(pairs):
                both_q[p] = two_heads(q[rows, lanes_of(q_at, p)], lane)

            def one_window(n, _):
                keys, bias = key_window(meta, kind, top, i, n, low, high)
                for p in range(pairs):
                    scores = dot_nt(k[keys, lanes_of(k_at, p)], both_q[p]) + bias
                    before = peaks[p : p + 1, :]
                    peak = jnp.maximum(before, jnp.max(scores, axis=0, keepdims=True))
                    fade = jnp.exp(before - peak)
                    weights = jnp.exp(scores - peak)
                    peaks[p : p + 1, :] = peak
                    totals[p : p + 1, :] = totals[p : p + 1, :] * fade + jnp.sum(weights, axis=0, keepdims=True)
                    mixed = both_blocks(dot_tn(v[keys, lanes_of(v_at, p)], weights.astype(bf16)))
                    faded = jnp.concatenate(
                        [jnp.broadcast_to(fade[:, :BLOCK], (64, BLOCK)), jnp.broadcast_to(fade[:, BLOCK:], (64, BLOCK))]
                    )
                    sums[p] = sums[p] * faded + mixed
                return 0

            lax.fori_loop(0, count, one_window, 0)
            for p in range(pairs):
                total = totals[p : p + 1, :]
                share = 1.0 / total
                shares = jnp.concatenate(
                    [jnp.broadcast_to(share[:, :BLOCK], (64, BLOCK)), jnp.broadcast_to(share[:, BLOCK:], (64, BLOCK))]
                )
                o[rows, lanes_of(0, p)] = (sums[p] * shares).T.astype(bf16)
                log_total = peaks[p : p + 1, :] + jnp.log(total)
                lse[2 * p : 2 * p + 1, rows] = log_total[:, :BLOCK]
                lse[2 * p + 1 : 2 * p + 2, rows] = log_total[:, BLOCK:]

        return 0

    lax.fori_loop(meta[0, FIRST], meta[0, LAST], one_block, 0)


def attend_back(meta, kind, top, info, info_row, q, k, v, lse, delta, do, dq, dk, dv, both_q, both_o, sums):
    (q, q_at), (k, k_at), (v, v_at), (dq, dq_at) = q, k, v, dq
    pairs = do.shape[1] // BLOCK

    def one_block(i, _):
        count = (meta[i, kind + 1] - meta[i, kind] + KEYS - 1) // KEYS

        @pl.when(count > 0)
        def _():
            rows = block(i)
            lane = lax.broadcasted_iota(i32, (BLOCK, BLOCK), 1)
            low, high = info[info_row : info_row + 1, rows], info[info_row + 1 : info_row + 2, rows]
            sums[...] = jnp.zeros(sums.shape, f32)
            for p in range(pairs):
                both_q[p] = two_heads(q[rows, lanes_of(q_at, p)], lane)
                both_o[p] = two_heads(do[rows, lanes_of(0, p)], lane)

            def one_window(n, _):
                keys, bias = key_window(meta, kind, top, i, n, low, high)
                for p in range(pairs):
                    lanes = lanes_of(0, p)
                    these = k[keys, lanes_of(k_at, p)]
                    queries, grads = both_q[p], both_o[p]
                    probs = jnp.exp(dot_nt(these, queries) + bias - two_rows(lse, p, rows))
                    grad_probs = dot_nt(v[keys, lanes_of(v_at, p)], grads)
                    grad_scores = (probs * (grad_probs - two_rows(delta, p, rows))).astype(bf16)
                    dv[keys, lanes] += dot(probs.astype(bf16), grads)
                    dk[keys, lanes] += dot(grad_scores, queries)
                    sums[p] += both_blocks(dot_tn(these, grad_scores))
                return 0

            lax.fori_loop(0, count, one_window, 0)
            for p in range(pairs):
                dq[rows, lanes_of(dq_at, p)] = (sums[p] * 0.125).T.astype(bf16)

        return 0

    lax.fori_loop(meta[0, FIRST], meta[0, LAST], one_block, 0)


def attention_forward_kernel(
    layer, meta, bank, x_in, mem_in, gain, go_rows, info,
    qkv_out, o1_out, l1, mid_out, q2_out, kv_out, o2_out, l2, final,
    x, mem, qkv, o1, mid, q2, kv, o2, out, wide, third, fourth, pairw, last, both_q, peaks, totals, sums, semaphores,
):
    length, width = x.shape
    kind, flag_m, top_m = 4 * layer, FLAG_M + 2 * layer, TOP_M + 2 * layer
    moves = Moves(meta, length, semaphores)
    section = 2 * layer
    x_here = moves.pair(x_in, x, FLAG_T)
    self_here = [moves.whole(bank.at[section, j], wide.at[:, j * width : (j + 1) * width]) for j in range(3)]
    mem_here = moves.pair(mem_in, mem, flag_m)
    pair_here = [moves.whole(bank.at[section, 5 + j], pairw.at[:, j * width : (j + 1) * width]) for j in range(2)]
    rest_here = [moves.whole(bank.at[section, j], place) for j, place in ((3, third), (4, fourth), (7, last))]
    go = (lambda rows: go_rows[rows, layer : layer + 1])
    x_here()
    for wait in self_here:
        wait()

    def self_in(rows, _):
        a = norm(x[rows, :].astype(f32), gain[0:1, :]).astype(bf16)
        both = dot(a, wide[...])
        qkv[rows, :width] = (both[:, :width] * 0.125).astype(bf16)
        qkv[rows, width:] = both[:, width:].astype(bf16)
        o1[rows, :] = jnp.zeros((rows.size, width), bf16)
        o2[rows, :] = jnp.zeros((rows.size, width), bf16)

    over(meta, FLAG_T, length, self_in)
    moves.away(qkv, qkv_out, FLAG_T)
    mem_here()
    for wait in pair_here:
        wait()

    def memory_in(rows, _):
        kv[rows, :] = dot(mem[rows, :], pairw[...]).astype(bf16)

    over(meta, flag_m, length, memory_in)
    moves.away(kv, kv_out, flag_m)
    l1[...] = jnp.zeros(l1.shape, f32)
    l2[...] = jnp.zeros(l2.shape, f32)
    attend(
        meta, SELF + kind, TOP_T, info, 0, (qkv, 0), (qkv, width), (qkv, 2 * width), o1, l1,
        both_q, peaks, totals, sums,
    )
    moves.away(o1, o1_out, FLAG_T)
    for wait in rest_here:
        wait()

    def cross_in(rows, _):
        state = x[rows, :].astype(f32) + go(rows) * dot(o1[rows, :], third[...])
        mid[rows, :] = state
        a = norm(state, gain[1:2, :]).astype(bf16)
        q2[rows, :] = (dot(a, fourth[...]) * 0.125).astype(bf16)

    over(meta, FLAG_T, length, cross_in)
    moves.away(mid, mid_out, FLAG_T)
    moves.away(q2, q2_out, FLAG_T)
    attend(
        meta, CROSS + kind, top_m, info, 2, (q2, 0), (kv, 0), (kv, width), o2, l2, both_q, peaks, totals, sums
    )
    moves.away(o2, o2_out, FLAG_T)

    def finish(rows, _):
        out[rows, :] = (mid[rows, :] + go(rows) * dot(o2[rows, :], last[...])).astype(bf16)

    over(meta, FLAG_T, length, finish)
    moves.away(out, final, FLAG_T)
    moves.finish()


def attention_backward_kernel(
    layer, meta, bank, x_in, mem_in, gain, go_rows, info,
    qkv_in, o1_in, l1, mid_in, q2_in, kv_in, o2_in, l2, dh_in, *rest,
):
    entry = layer == 0
    if entry:
        dmem_in, *rest = rest
    (
        dx_out, dmem_out, dw_out, dgain,
        x, mem, qkv, o1, mid, q2, kv, o2, dh, dx, dmem, dw,
        wide, third, fourth, pairw, last,
        dstate, do, dqkv, dk, dv, delta, heads, both_q, both_o, sums, acc, semaphores,
    ) = rest
    length, width = x.shape
    kind, flag_m, top_m = 4 * layer, FLAG_M + 2 * layer, TOP_M + 2 * layer
    moves = Moves(meta, length, semaphores)
    section = 2 * layer
    first_here = [
        moves.pair(dh_in, dh, FLAG_T), moves.whole(bank.at[section, 7], last), moves.pair(o2_in, o2, FLAG_T),
        moves.pair(q2_in, q2, FLAG_T), moves.pair(kv_in, kv, flag_m),
    ]
    if entry:
        first_here.append(moves.whole(dmem_in, dmem))
    second_here = [moves.pair(mem_in, mem, flag_m), moves.pair(mid_in, mid, FLAG_T)]
    second_here += [moves.whole(bank.at[section, 5 + j], pairw.at[:, j * width : (j + 1) * width]) for j in range(2)]
    second_here += [moves.whole(bank.at[section, 4], fourth)]
    third_here = [moves.whole(bank.at[section, 3], third), moves.pair(o1_in, o1, FLAG_T), moves.pair(qkv_in, qkv, FLAG_T)]
    fourth_here = [moves.whole(bank.at[section, j], wide.at[:, j * width : (j + 1) * width]) for j in range(3)]
    fourth_here += [moves.pair(x_in, x, FLAG_T)]
    go = (lambda rows: go_rows[rows, layer : layer + 1])

    row_of = lax.broadcasted_iota(i32, (HEADS, width), 0)
    lane_of = lax.broadcasted_iota(i32, (HEADS, width), 1)
    heads[...] = (lane_of // (width // HEADS) == row_of).astype(bf16)
    dk[...] = jnp.zeros(dk.shape, f32)
    dv[...] = jnp.zeros(dv.shape, f32)
    delta[...] = jnp.zeros(delta.shape, f32)
    if not entry:
        dmem[...] = jnp.zeros(dmem.shape, bf16)
    if entry:
        dx[...] = jnp.zeros(dx.shape, bf16)

    def weight_grad(targets, flag, left, right):
        size = len(targets) * width

        def part(rows, fresh):
            term = dot_tn(left(rows), right(rows))
            acc[:, :size] = term if fresh else acc[:, :size] + term

        over(meta, flag, length, part)
        for n, j in enumerate(targets):
            dw[j] = acc[:, n * width : (n + 1) * width].astype(bf16)
            moves.away(dw.at[j], dw_out.at[j])

    def begin(grad_of, o, out_weight, target):
        def dy(rows):
            return (go(rows) * grad_of(rows)).astype(bf16)

        def part(rows, _):
            grad = dot_nt(dy(rows), out_weight[...]).astype(bf16)
            do[rows, :] = grad
            product = grad.astype(f32) * o[rows, :].astype(f32)
            high = product.astype(bf16)
            rest = (product - high.astype(f32)).astype(bf16)
            delta[:, rows] = dot_nt(heads[...], high) + dot_nt(heads[...], rest)
            dqkv[rows, :width] = jnp.zeros((rows.size, width), bf16)

        over(meta, FLAG_T, length, part)
        weight_grad([target], FLAG_T, lambda rows: o[rows, :], dy)

    def top_grad(rows):
        return dh[rows, :].astype(f32)

    for wait in first_here:
        wait()
    begin(top_grad, o2, last, 7)
    attend_back(
        meta, CROSS + kind, top_m, info, 2, (q2, 0), (kv, 0), (kv, width), l2, delta, do, (dqkv, 0), dk, dv,
        both_q, both_o, sums,
    )
    for wait in second_here:
        wait()

    def memory_out(rows, _):
        dqkv[rows, width : 2 * width] = dk[rows, :].astype(bf16)
        dqkv[rows, 2 * width :] = dv[rows, :].astype(bf16)
        term = dot_nt(dqkv[rows, width:], pairw[...])
        dmem[rows, :] = (dmem[rows, :].astype(f32) + term).astype(bf16)

    over(meta, flag_m, length, memory_out)
    moves.away(dmem, dmem_out)
    weight_grad([5, 6], flag_m, lambda rows: mem[rows, :], lambda rows: dqkv[rows, width:])

    def cross_out(rows, fresh):
        grad_x, grad_gain = norm_back(mid[rows, :], gain[1:2, :], dot_nt(dqkv[rows, :width], fourth[...]))
        dstate[rows, :] = top_grad(rows) + grad_x
        dgain[1:2, :] = grad_gain if fresh else dgain[1:2, :] + grad_gain

    over(meta, FLAG_T, length, cross_out)
    weight_grad(
        [4], FLAG_T, lambda rows: norm(mid[rows, :], gain[1:2, :]).astype(bf16), lambda rows: dqkv[rows, :width]
    )
    for wait in third_here:
        wait()
    dk[...] = jnp.zeros(dk.shape, f32)
    dv[...] = jnp.zeros(dv.shape, f32)
    begin(lambda rows: dstate[rows, :], o1, third, 3)
    attend_back(
        meta, SELF + kind, TOP_T, info, 0, (qkv, 0), (qkv, width), (qkv, 2 * width), l1, delta, do, (dqkv, 0), dk, dv,
        both_q, both_o, sums,
    )
    for wait in fourth_here:
        wait()

    def self_out(rows, fresh):
        dqkv[rows, width : 2 * width] = dk[rows, :].astype(bf16)
        dqkv[rows, 2 * width :] = dv[rows, :].astype(bf16)
        grad_x, grad_gain = norm_back(x[rows, :].astype(f32), gain[0:1, :], dot_nt(dqkv[rows, :], wide[...]))
        value = dstate[rows, :] + grad_x
        if entry:
            value = jnp.where(go_rows[rows, 2:3] > 0.0, value, 0.0)
        dx[rows, :] = value.astype(bf16)
        dgain[0:1, :] = grad_gain if fresh else dgain[0:1, :] + grad_gain

    over(meta, FLAG_T, length, self_out)
    if entry:
        moves.away(dx, dx_out)
    else:
        moves.away(dx, dx_out, FLAG_T)
    weight_grad(
        [0, 1, 2], FLAG_T, lambda rows: norm(x[rows, :].astype(f32), gain[0:1, :]).astype(bf16),
        lambda rows: dqkv[rows, :],
    )
    moves.finish()


def exit_part(layer, vector, frows, rows, target_row, halt, exit_grad, fresh, sentences):
    factor = layer.shape[1] ** (-0.5)
    vectors = jnp.broadcast_to(vector, (8, layer.shape[1]))
    score = jax.nn.sigmoid(exact_nt(vectors, layer) * factor)
    halt[:, rows] = score
    weight = frows[0:1, rows] * (score - frows[target_row : target_row + 1, rows]) / sentences
    term = exact(weight, layer)[0:1] * factor
    exit_grad[...] = term if fresh else exit_grad[...] + term


def dense_weights(moves, bank, section, up, down, width):
    parts = up.shape[1] // width
    here = [moves.whole(bank.at[section, j], up.at[:, j * width : (j + 1) * width]) for j in range(parts)]
    later = [moves.whole(bank.at[section, parts + j], down.at[j * width : (j + 1) * width]) for j in range(parts)]
    return here, later


def dense_forward_kernel(
    sentences, meta, bank, x, gain, frows, final, halt, exit_grad, out, up, down, semaphores
):
    length, width = x.shape
    moves = Moves(meta, length, semaphores)
    here, later = dense_weights(moves, bank, 1, up, down, width)
    for wait in here:
        wait()

    def part(rows, fresh):
        state = x[rows, :].astype(f32)
        a = norm(state, gain[0:1, :]).astype(bf16)
        active = gelu(dot(a, up[...])).astype(bf16)
        if fresh:
            for wait in later:
                wait()
        layer = state + dot(active, down[...])
        out[rows, :] = layer.astype(bf16)
        exit_part(layer, gain[1:2, :], frows, rows, 1, halt, exit_grad, fresh, sentences)

    over(meta, FLAG_T, length, part)
    moves.away(out, final, FLAG_T)
    moves.finish()


def dense_backward_kernel(sentences, final, meta, bank, x, gain, go_rows, frows, dh, before, dx_out, dw_out, dgain, *rest):
    if final:
        states, halt, exit_grad, out, *rest = rest
        out[...] = jnp.zeros(out.shape, bf16)
    else:
        dgain[1:2, :] = before[...]
    dx, dw, up, down, grad_up, grad_down, semaphores = rest
    length, width = x.shape
    moves = Moves(meta, length, semaphores)
    here, later = dense_weights(moves, bank, 3 if final else 1, up, down, width)
    parts = up.shape[1] // width
    for wait in here:
        wait()

    def part(rows, fresh):
        grad_out = dh[rows, :].astype(f32)
        if final:
            grad_out = jnp.where(go_rows[rows, 2:3] > 0.0, grad_out, 0.0)
        go = go_rows[rows, int(final) : int(final) + 1]
        state = x[rows, :].astype(f32)
        a = norm(state, gain[0:1, :]).astype(bf16)
        dy = (go * grad_out).astype(bf16)
        active, slope = gelu_both(dot(a, up[...]))
        active = active.astype(bf16)
        if fresh:
            for wait in later:
                wait()
        dhidden = (slope * dot_nt(dy, down[...])).astype(bf16)
        downs, ups = dot_tn(active, dy), dot_tn(a, dhidden)
        if fresh:
            grad_down[...] = downs
            grad_up[...] = ups
        else:
            grad_down[...] += downs
            grad_up[...] += ups
        if final:
            layer = state + go * dot(active, down[...])
            out[rows, :] = jnp.where(go_rows[rows, 2:3] > 0.0, layer, 0.0).astype(bf16)
            exit_part(layer, gain[1:2, :], frows, rows, 2, halt, exit_grad, fresh, sentences)
        grad_x, grad_gain = norm_back(state, gain[0:1, :], dot_nt(dhidden, up[...]))
        dx[rows, :] = (grad_out + grad_x).astype(bf16)
        dgain[0:1, :] = grad_gain if fresh else dgain[0:1, :] + grad_gain

    over(meta, FLAG_T, length, part)
    moves.away(dx, dx_out, FLAG_T)
    if final:
        moves.away(out, states)
        dgain[1:2, :] = exit_grad[...]
        mine = frows[3:4, :] > 0.0
        halt[1:2, :] = jnp.where(mine, halt[1:2, :], 0.0)
        halt[0:1, :] = jnp.where(mine, before[0:1, :], 0.0)
    for j in range(parts):
        dw[parts + j] = grad_down[j * width : (j + 1) * width, :].astype(bf16)
        dw[j] = grad_up[:, j * width : (j + 1) * width].astype(bf16)
        moves.away(dw.at[j], dw_out.at[j])
        moves.away(dw.at[parts + j], dw_out.at[parts + j])
    moves.finish()


def plan_kernel(sentences, row, core, seg, pad, mseg, mmask, depths, meta, info, frows, cols):
    row, core = row[0], core[0]
    length, slots = seg.shape[1], mseg.shape[1]
    blocks = length // BLOCK
    seg, pad, mseg, mmask = (t[pl.ds(row, 1), :] for t in (seg, pad, mseg, mmask))
    number = lax.broadcasted_iota(i32, (sentences, length), 0)
    place = lax.broadcasted_iota(i32, (1, length), 1)

    def count(marks):
        return jnp.sum(marks.astype(f32), axis=1, keepdims=True).astype(i32)

    square = lax.broadcasted_iota(i32, (sentences, sentences), 0) == lax.broadcasted_iota(
        i32, (sentences, sentences), 1
    )
    depth_row = jnp.broadcast_to(depths[pl.ds(row, 1), :], (sentences, sentences))
    depth_table = jnp.sum(jnp.where(square, depth_row, 0).astype(f32), axis=1, keepdims=True).astype(i32)
    mine = seg == number
    starts = count(seg < number)
    filled = count(pad == 1)
    memory_number = lax.broadcasted_iota(i32, (sentences, slots), 0)
    memory_starts = count(mseg < memory_number)
    memory_stops = jnp.minimum(count(mseg <= memory_number), count(mmask == 1))

    def of_token(table):
        return jnp.sum(jnp.where(mine, table, 0), axis=0, keepdims=True)

    low = of_token(starts)
    high = jnp.where(pad == 1, jnp.minimum(place, filled - 1), place) + 1
    cross_low = jnp.where(pad == 0, 0, of_token(memory_starts))
    cross_high = jnp.where(pad == 0, slots, of_token(memory_stops))
    depth = of_token(depth_table)
    keep = depth == 2

    later = lax.broadcasted_iota(i32, (sentences, 1), 0) > 0
    away = jnp.where(later, jnp.abs(starts - length // 2), length)
    nearest = jnp.min(away, axis=0, keepdims=True)
    cut = jnp.min(jnp.where(away == nearest, starts, length), axis=0, keepdims=True)

    def by_core(first, second):
        return first * (1 - core) + second * core

    below = jnp.where(place < cut, 1, 0)
    owned = by_core(below, 1 - below) == 1
    begin = by_core(0, cut // BLOCK)
    end = by_core((cut + BLOCK - 1) // BLOCK, blocks)
    wide = length * 5 // 8
    base = by_core(0, length - wide)

    def outside(from_place, to_place):
        return by_core(jnp.where(to_place > wide, 1, 0), jnp.where(from_place < length - wide, 1, 0))

    def top_of(flag):
        return jnp.where(flag == 1, length - KEYS, base + wide - KEYS)

    def by_block(values):
        return jnp.concatenate([values[:, i * BLOCK : (i + 1) * BLOCK] for i in range(blocks)], axis=0)

    lane = lax.broadcasted_iota(i32, (blocks, 128), 1)
    table = jnp.zeros((blocks, 128), i32)
    flag_t = outside(begin * BLOCK, end * BLOCK)
    entries = {CORE: jnp.full((1, 1), core, i32), FLAG_T: flag_t, FIRST: begin, LAST: end, TOP_T: top_of(flag_t)}
    for layer in range(2):
        used = owned if layer == 0 else owned & keep
        for kind, lows, highs in ((SELF, low, high), (CROSS, cross_low, cross_high)):
            lows = jnp.min(by_block(jnp.where(used, lows, slots)), axis=1, keepdims=True)
            highs = jnp.max(by_block(jnp.where(used, highs, 0)), axis=1, keepdims=True)
            entries[kind + 4 * layer] = jnp.minimum(lows, highs) // STEP * STEP
            entries[kind + 4 * layer + 1] = highs
        flag_m = outside(
            jnp.min(jnp.where(used, cross_low, slots), axis=1, keepdims=True),
            jnp.max(jnp.where(used, cross_high, 0), axis=1, keepdims=True),
        )
        entries[FLAG_M + 2 * layer] = flag_m
        entries[TOP_M + 2 * layer] = top_of(flag_m)
    for column, values in entries.items():
        table = jnp.where(lane == column, values, table)
    meta[...] = table
    info[...] = jnp.concatenate([low, high, cross_low, cross_high, low, low, low, low], axis=0)
    ones = jnp.ones((1, length), f32)
    kept, own = keep.astype(f32), owned.astype(f32)
    counted = jnp.where(pad == 1, own, 0.0)
    frows[...] = jnp.concatenate([counted, (depth == 1).astype(f32), ones, own, ones, ones, ones, ones], axis=0)
    by_row = jnp.concatenate([ones, kept, own, own, own, own, own, own], axis=0)
    for i in range(blocks):
        cols[i * BLOCK : (i + 1) * BLOCK, :] = by_row[:, i * BLOCK : (i + 1) * BLOCK].T


ANY = pl.BlockSpec(memory_space=pl.ANY)
VMEM = pl.BlockSpec(memory_space=pltpu.VMEM)
SMEM = pl.BlockSpec(memory_space=pltpu.SMEM)


def make_plan(row, core, ints):
    seg, pad, mseg, mmask, depths = ints
    length, sentences = seg.shape[1], depths.shape[1]
    outs = [((length // BLOCK, 128), i32), ((8, length), i32), ((8, length), f32), ((length, 8), f32)]
    return pl.pallas_call(
        functools.partial(plan_kernel, sentences),
        out_shape=[jax.ShapeDtypeStruct(*out) for out in outs],
        in_specs=[SMEM, SMEM] + [VMEM] * 5,
        out_specs=[VMEM] * 4,
        name="make_plan",
    )(row.astype(i32)[None], core.astype(i32)[None], seg, pad, mseg, mmask, depths)


def run(kernel, ins, outs, scratch, semaphores, name, flops, *args):
    return pl.pallas_call(
        kernel,
        out_shape=[jax.ShapeDtypeStruct(shape, dtype) for _, shape, dtype in outs],
        in_specs=ins,
        out_specs=[spec for spec, _, _ in outs],
        scratch_shapes=[pltpu.VMEM(shape, dtype) for shape, dtype in scratch]
        + [pltpu.SemaphoreType.DMA((semaphores,))],
        compiler_params=pltpu.CompilerParams(vmem_limit_bytes=60 * 2**20),
        cost_estimate=pl.CostEstimate(flops=flops, bytes_accessed=20 * 2**20, transcendentals=0),
        name=name,
    )(*args)


def attention_forward(layer, plan, bank, x, mem, gain, name):
    meta, info, _, cols = plan
    length, width = x.shape
    pairs = width // BLOCK

    def rows(n, dtype=bf16):
        return ((length, n * width), dtype)

    logs = (VMEM, (HEADS, length), f32)
    kept = [rows(3), rows(1), logs[1:], rows(1, f32), rows(1), rows(2), rows(1), logs[1:], rows(1)]
    outs = [(VMEM if shape[0] == HEADS else ANY, shape, dtype) for shape, dtype in kept]
    square = ((width, width), bf16)
    scratch = [
        rows(1), rows(1), rows(3), rows(1), rows(1, f32), rows(1), rows(2), rows(1), rows(1),
        ((width, 3 * width), bf16), square, square, ((width, 2 * width), bf16), square,
        ((pairs, 2 * BLOCK, BLOCK), bf16), ((8, 2 * BLOCK), f32), ((8, 2 * BLOCK), f32), ((pairs, BLOCK, BLOCK), f32),
    ]
    return run(
        functools.partial(attention_forward_kernel, layer), [SMEM, ANY, ANY, ANY, VMEM, VMEM, VMEM], outs, scratch, 32,
        name, 6 * 10**9, meta, bank, x, mem, gain, cols, info,
    )


def attention_backward(layer, plan, bank, x, mem, gain, saved, dh, dmem, name):
    meta, info, _, cols = plan
    length, width = x.shape
    pairs = width // BLOCK

    def rows(n, dtype=bf16):
        return ((length, n * width), dtype)

    square, matrices = ((width, width), bf16), (bank.shape[1:], bf16)
    outs = [(ANY, *rows(1)), (ANY, *rows(1)), (ANY, *matrices), (VMEM, (2, width), f32)]
    both = ((pairs, 2 * BLOCK, BLOCK), bf16)
    scratch = [
        rows(1), rows(1), rows(3), rows(1), rows(1, f32), rows(1), rows(2), rows(1), rows(1), rows(1), rows(1), matrices,
        ((width, 3 * width), bf16), square, square, ((width, 2 * width), bf16), square,
        rows(1, f32), rows(1), rows(3), rows(1, f32), rows(1, f32), ((HEADS, length), f32), ((HEADS, width), bf16),
        both, both, ((pairs, BLOCK, BLOCK), f32), ((width, 3 * width), f32),
    ]
    ins = [SMEM, ANY, ANY, ANY, VMEM, VMEM, VMEM, ANY, ANY, VMEM, ANY, ANY, ANY, ANY, VMEM, ANY] + [ANY] * len(dmem)
    return run(
        functools.partial(attention_backward_kernel, layer), ins, outs, scratch, 48,
        name, 12 * 10**9, meta, bank, x, mem, gain, cols, info, *saved, dh, *dmem,
    )


def dense_forward(plan, bank, x, gain, sentences, name):
    meta, _, frows, _ = plan
    length, width = x.shape
    wide = ((length, width), bf16)
    hidden = bank.shape[1] // 2 * width
    outs = [(ANY, *wide), (VMEM, (8, length), f32), (VMEM, (1, width), f32)]
    return run(
        functools.partial(dense_forward_kernel, sentences), [SMEM, ANY, VMEM, VMEM, VMEM], outs,
        [wide, ((width, hidden), bf16), ((hidden, width), bf16)], 16,
        name, 4 * 10**9, meta, bank, x, gain, frows,
    )


def dense_backward(plan, bank, x, gain, dh, before, sentences, final, name):
    meta, _, frows, cols = plan
    length, width = x.shape
    wide = ((length, width), bf16)
    hidden = bank.shape[1] // 2 * width
    outs = [(ANY, *wide), (ANY, bank.shape[1:], bf16), (VMEM, (2, width), f32)]
    scratch = [wide, (bank.shape[1:], bf16), ((width, hidden), bf16), ((hidden, width), bf16),
               ((width, hidden), f32), ((hidden, width), f32)]
    if final:
        outs += [(ANY, *wide), (VMEM, (8, length), f32)]
        scratch = [((1, width), f32), wide] + scratch
    return run(
        functools.partial(dense_backward_kernel, sentences, final), [SMEM, ANY] + [VMEM] * 6, outs, scratch, 24,
        name, 8 * 10**9, meta, bank, x, gain, cols, frows, dh, before,
    )


def row_forward_backward(row, core, x, mem, cotangent, bank, gains, ints):
    plan = make_plan(row, core, ints)
    sentences = ints[-1].shape[1]
    *saved0, zero = attention_forward(0, plan, bank, x, mem, gains[0], "attend_zero")
    one, halt, exit0 = dense_forward(plan, bank, zero, gains[1], sentences, "dense_one")
    *saved2, two = attention_forward(1, plan, bank, one, mem, gains[2], "attend_two")
    dtwo, dw3, dgain3, states, halt = dense_backward(
        plan, bank, two, gains[3], cotangent, halt, sentences, True, "dense_three"
    )
    done, dmem, dw2, dgain2 = attention_backward(1, plan, bank, one, mem, gains[2], saved2, dtwo, (), "attend_two_back")
    dzero, dw1, dgain1 = dense_backward(plan, bank, zero, gains[1], done, exit0, sentences, False, "dense_one_back")
    dx, dmem, dw0, dgain0 = attention_backward(
        0, plan, bank, x, mem, gains[0], saved0, dzero, (dmem,), "attend_zero_back"
    )
    return states, halt, dx, dmem, [dw0, dw1, dw2, dw3], [dgain0, dgain1, dgain2, dgain3]


MESH = pl.DeviceIdType.MESH


def neighbours():
    s, d = lax.axis_index("section"), lax.axis_index("dp")
    across = [(s + 1 - 2 * (s % 2), d), ((s + 2) % 4, d), (3 - s, d)]
    layer = d // 2
    along = (s, d + 2 - 4 * (layer % 2))
    sibling = (s, d + 1 - 2 * (d % 2))
    return s, d, across, along, sibling


def greet(devices):
    barrier = pltpu.get_barrier_semaphore()
    for device in devices:
        pl.semaphore_signal(barrier, inc=1, device_id=device, device_id_type=MESH)
    pl.semaphore_wait(barrier, len(devices))


SUBS = 4


def gather_kernel(
    states, memory, cotangent, bank, gains, seg, pad, mseg, mmask, depths,
    x, mem, top, weights, gains_all, seg2, pad2, mseg2, mmask2, depths2,
    staging, send, recv, home,
):
    s, d, across, along, sibling = neighbours()
    core = d % 2
    parity = (d // 2) % 2
    greet(across + [along, sibling])
    started = []
    locals_ = []
    count = [0, 0]

    def push(src, dst, device):
        i = count[0]
        count[0] += 1
        copy = pltpu.make_async_remote_copy(src, dst, send.at[i], recv.at[i], device_id=device, device_id_type=MESH)
        return copy

    def go(src, dst, device):
        copy = push(src, dst, device)
        copy.start()
        started.append(copy)
        return copy

    def keep(src, dst):
        i = count[1]
        count[1] += 1
        copy = pltpu.make_async_copy(src, dst, home.at[i])
        return copy

    shares = states.shape[2]
    chips = [s] + [a[0] for a in across]
    sent_inputs, own_inputs = [], []
    for source, whole in ((states, x), (memory, mem), (cotangent, top)):
        for rel in range(4):
            target = chips[rel]
            mine = target // 2 == core
            dst = whole.at[:, pl.ds(pl.multiple_of(s * shares, shares), shares)]
            src = source.at[target % 2]
            if rel == 0:
                copy = keep(src, dst)
                own_inputs.append(copy)
            else:
                copy = push(src, dst, across[rel - 1])
                sent_inputs.append((copy, whole, rel))
            pl.when(mine)(copy.start)
    small = [go(source, whole.at[core], sibling)
             for source, whole in ((seg, seg2), (pad, pad2), (mseg, mseg2), (mmask, mmask2), (depths, depths2))]
    small += [go(gains, gains_all.at[s], device) for device in across]
    for source, whole in ((seg, seg2), (pad, pad2), (mseg, mseg2), (mmask, mmask2), (depths, depths2)):
        copy = keep(source, whole.at[core])
        copy.start()
        locals_.append(copy)
    copy = keep(gains, gains_all.at[s])
    copy.start()
    locals_.append(copy)

    span = bank.shape[0]
    half = span // 2
    third = half // 3 // (16 * SUBS) * (16 * SUBS)
    first = half - 2 * third
    sub0, sub1 = first // SUBS, third // SUBS

    def rows(section, part, i):
        at = section * span + core * half
        size = sub0 if part == 0 else sub1
        if part == 0:
            at = at + i * size
        elif part == 1:
            at = at + first + parity * third + i * size
        else:
            at = at + first + (1 - parity) * third + i * size
        return weights.at[pl.ds(pl.multiple_of(at, 16), size)]

    def own_rows(part, i):
        size = sub0 if part == 0 else sub1
        at = core * half + (i * size if part == 0 else first + parity * third + i * size)
        return bank.at[pl.ds(pl.multiple_of(at, 16), size)]

    direct = {}
    for part in (1, 0):
        for i in range(SUBS):
            for k in range(2):
                direct[k, part, i] = go(own_rows(part, i), rows(s, part, i), across[k])
    lift = keep(bank, staging)
    lift.start()
    drop = keep(staging, weights.at[pl.ds(pl.multiple_of(s * span, span), span)])

    holder = s // 2 == core
    handed = []
    for n, (source, whole) in enumerate(((states, x), (memory, mem), (cotangent, top))):
        for rel in range(4):
            lanes = whole.at[:, pl.ds(pl.multiple_of(chips[rel] * shares, shares), shares)]
            copy = push(lanes, lanes, sibling)
            handed.append(copy)
            arrived = own_inputs[n] if rel == 0 else sent_inputs[n * 3 + rel - 1][0]

            def hand(copy=copy, arrived=arrived, rel=rel):
                if rel == 0:
                    arrived.wait()
                else:
                    arrived.wait_recv()
                copy.start()

            pl.when(holder)(hand)

    lift.wait()
    drop.start()
    locals_.append(drop)
    far = {}
    lifted = {}
    passed = []

    def arrive(copy, section, part, i):
        copy.wait_recv()
        passed.append(go(rows(section, part, i), rows(section, part, i), sibling))

    for i in range(SUBS):
        arrive(direct[0, 1, i], chips[1], 1, i)
        far[1, i] = go(rows(chips[1], 1, i), rows(chips[1], 1, i), across[1])
        lifted[1, i] = go(rows(chips[1], 1, i), rows(chips[1], 1, i), along)
        arrive(direct[1, 1, i], chips[2], 1, i)
        lifted[2, i] = go(rows(chips[2], 1, i), rows(chips[2], 1, i), along)
    for i in range(SUBS):
        arrive(direct[1, 0, i], chips[2], 0, i)
        far[0, i] = go(rows(chips[2], 0, i), rows(chips[2], 0, i), across[0])
        arrive(direct[0, 0, i], chips[1], 0, i)
    for i in range(SUBS):
        arrive(far[1, i], chips[3], 1, i)
        lifted[3, i] = go(rows(chips[3], 1, i), rows(chips[3], 1, i), along)
    for i in range(SUBS):
        arrive(far[0, i], chips[3], 0, i)
    for k in range(1, 4):
        for i in range(SUBS):
            arrive(lifted[k, i], chips[k], 2, i)
    for copy in passed + small:
        copy.wait_recv()
    for copy in handed:
        pl.when(jnp.logical_not(holder))(copy.wait_recv)
        pl.when(holder)(copy.wait_send)
    for (copy, whole, rel) in sent_inputs:
        pl.when(chips[rel] // 2 == core)(copy.wait_send)
    for copy in started:
        copy.wait_send()
    for copy in locals_:
        copy.wait()


def gather_all(states, memory, cotangent, bank, gains, ints):
    micro, length, shares = states.shape
    sections = lax.axis_size("section")
    width = shares * sections
    wide = jax.ShapeDtypeStruct((length, width), bf16)
    copies = 9 + 12 + 8 + 4 * SUBS + 2 * SUBS + 3 * SUBS + 9 * SUBS
    outs = [wide, wide, wide, jax.ShapeDtypeStruct((sections * bank.shape[0], width), bf16),
            jax.ShapeDtypeStruct((sections,) + gains.shape, f32)]
    outs += [jax.ShapeDtypeStruct((2,) + t.shape, t.dtype) for t in ints]
    return pl.pallas_call(
        gather_kernel,
        out_shape=outs,
        in_specs=[ANY] * 10,
        out_specs=[ANY] * 10,
        scratch_shapes=[pltpu.VMEM(bank.shape, bank.dtype), pltpu.SemaphoreType.DMA((copies,)), pltpu.SemaphoreType.DMA((copies,)),
                        pltpu.SemaphoreType.DMA((12,))],
        compiler_params=pltpu.CompilerParams(collective_id=0, has_side_effects=True, vmem_limit_bytes=16 * 2**20),
        name="gather_all",
    )(states, memory, cotangent, bank, gains, *ints)


GROUPS = 8
AHEAD = 2
RESULTS = 7


def add_rows(target, rows, *others):
    total = target[rows].astype(f32)
    for other, places in others:
        total = total + other[places].astype(f32)
    target[rows] = total.astype(bf16)


def reduce_kernel(
    dw0, dw1, dw2, dw3, gains, states, dx, dmem, halt,
    bank, gains_sum, states_out, dx_out, dmem_out, halt_out,
    own, other, first, second, left, right, total, full, mine, theirs, score, scores,
    gain_parts, send, recv, home,
):
    s, d, across, _, sibling = neighbours()
    core, layer = d % 2, d // 2
    chips = [s] + [a[0] for a in across]
    column = [(s, (layer + k) % 4 * 2 + core) for k in range(1, 4)]
    up, down = (s, d + 2), (s, d - 2)
    pair = (s, d + 2 - 4 * (layer % 2))
    jump = (s, (layer + 2) % 4 * 2 + core)
    holder = s // 2 == core
    greet(across + [sibling] + column)
    count = [0, 0]
    always, ends = [], []

    def push(src, dst, device):
        i = count[0]
        count[0] += 1
        return pltpu.make_async_remote_copy(src, dst, send.at[i], recv.at[i], device_id=device, device_id_type=MESH)

    def go(src, dst, device):
        copy = push(src, dst, device)
        copy.start()
        always.append(copy)
        return copy

    def fetch(src, dst):
        i = count[1]
        count[1] += 1
        copy = pltpu.make_async_copy(src, dst, home.at[i])
        return copy

    span = dw0.shape[0]
    half = span // 2
    quarter = half // 2
    piece = quarter // GROUPS
    grads = (dw0, dw1, dw2, dw3)

    def at(g, side):
        return side * quarter + g * piece

    loads, swaps = {}, {}

    def exchange(g):
        for t in range(4):
            for side in range(2):
                rows = pl.ds(at(g, side), piece)
                there = pl.ds(pl.multiple_of((1 - core) * half + at(g, side), piece), piece)
                here = pl.ds(pl.multiple_of(core * half + at(g, side), piece), piece)
                swaps[g, t, side] = go(grads[t].at[there], other.at[t, rows], sibling)
                loads[g, t, side] = fetch(grads[t].at[here], own.at[t, rows])
                loads[g, t, side].start()

    for g in range(AHEAD):
        exchange(g)
    outs = ((states, states_out), (dx, dx_out), (dmem, dmem_out))
    given, taken = [], []
    for n, (source, _) in enumerate(outs):
        given.append(push(source, theirs.at[n], sibling))
        taken.append(fetch(source, mine.at[n]))
    given.append(push(halt, scores, sibling))
    taken.append(fetch(halt, score))

    def results_begin():
        for copy in given:
            pl.when(jnp.logical_not(holder))(copy.start)
        for copy in taken:
            pl.when(holder)(copy.start)

    gain_steps = [sibling, across[0], across[1], pair, jump]
    gain_parts[0] = gains[...]
    gain_copies = []

    def gain_step(k):
        if k > 0:
            gain_copies[-1].wait_recv()
            gain_parts[2 * k] = gain_parts[2 * k - 2] + gain_parts[2 * k - 1]
        if k < len(gain_steps):
            gain_copies.append(go(gain_parts.at[2 * k], gain_parts.at[2 * k + 1], gain_steps[k]))
        else:
            gains_sum[...] = gain_parts[2 * k]

    step1, step2, rs, ag = {}, {}, {}, {}

    def plane_first(g):
        if g + AHEAD < GROUPS:
            exchange(g + AHEAD)
        for t in range(4):
            for side in range(2):
                swaps[g, t, side].wait_recv()
                loads[g, t, side].wait()
                rows = pl.ds(at(g, side), piece)
                add_rows(own, (t, rows), (other, (t, rows)))
        for side in range(2):
            rows = pl.ds(at(g, side), piece)
            for n, rel in enumerate((3, 1 + side)):
                step1[g, side, n] = go(own.at[chips[rel], rows], first.at[g, side, n], across[side])

    def plane_second(g):
        for side in range(2):
            rows = pl.ds(at(g, side), piece)
            for n, rel in enumerate((2 - side, 0)):
                step1[g, side, n].wait_recv()
                add_rows(own, (chips[rel], rows), (first, (g, side, n)))
                if n == 0:
                    step2[g, side] = go(own.at[chips[rel], rows], second.at[g, side], across[1 - side])

    def plane_third(g):
        for side in range(2):
            step2[g, side].wait_recv()
            rows = pl.ds(at(g, side), piece)
            value = own[s, rows].astype(f32) + second[g, side].astype(f32)
            total[g, pl.ds(side * piece, piece)] = value.astype(bf16)

    wide = 2 * piece
    shard = wide // 4

    def span_of(k0, k1):
        return pl.ds(k0 * shard, (k1 - k0) * shard)

    def share(kind, g, low, high, src, dst, device):
        return push(src.at[g, span_of(low, high)], dst.at[g, span_of(low, high)], device)

    def line_sums(g):
        for z in range(3):
            rs[g, "up", z] = share("up", g, z + 1, 4, total, right, up)
            rs[g, "down", z + 1] = share("down", g, 0, z + 1, total, left, down)
        for k in range(4):
            for z in range(k, 3):
                ag[g, "up", z, k] = push(full.at[g, span_of(k, k + 1)], full.at[g, span_of(k, k + 1)], up)
            for z in range(1, k + 1):
                ag[g, "down", z, k] = push(full.at[g, span_of(k, k + 1)], full.at[g, span_of(k, k + 1)], down)

    def at_layer(z, action):
        pl.when(layer == z)(action)

    def close(g, k, *others):
        value = total[g, span_of(k, k + 1)].astype(f32)
        for other_ in others:
            value = value + other_[g, span_of(k, k + 1)].astype(f32)
        full[g, span_of(k, k + 1)] = value.astype(bf16)

    def line_1(g):
        line_sums(g)
        at_layer(0, lambda: rs[g, "up", 0].start())
        at_layer(3, lambda: rs[g, "down", 3].start())

    def line_2(g):
        def second_layer():
            rs[g, "up", 0].wait_recv()
            add_rows(total, (g, span_of(2, 4)), (right, (g, span_of(2, 4))))
            rs[g, "up", 1].start()

        def third_layer():
            rs[g, "down", 3].wait_recv()
            add_rows(total, (g, span_of(0, 2)), (left, (g, span_of(0, 2))))
            rs[g, "down", 2].start()

        at_layer(1, second_layer)
        at_layer(2, third_layer)

    def line_3(g):
        def third_layer():
            rs[g, "up", 1].wait_recv()
            add_rows(total, (g, span_of(3, 4)), (right, (g, span_of(3, 4))))
            rs[g, "up", 2].start()
            close(g, 2, right, left)
            ag[g, "up", 2, 2].start()
            ag[g, "down", 2, 2].start()

        def second_layer():
            rs[g, "down", 2].wait_recv()
            add_rows(total, (g, span_of(0, 1)), (left, (g, span_of(0, 1))))
            rs[g, "down", 1].start()
            close(g, 1, right, left)
            ag[g, "up", 1, 1].start()
            ag[g, "down", 1, 1].start()

        at_layer(2, third_layer)
        at_layer(1, second_layer)

    def line_4(g):
        def bottom():
            rs[g, "down", 1].wait_recv()
            close(g, 0, left)
            ag[g, "up", 0, 0].start()

        def top():
            rs[g, "up", 2].wait_recv()
            close(g, 3, right)
            ag[g, "down", 3, 3].start()

        def second_layer():
            ag[g, "down", 2, 2].wait_recv()
            ag[g, "down", 1, 2].start()

        def third_layer():
            ag[g, "up", 1, 1].wait_recv()
            ag[g, "up", 2, 1].start()

        at_layer(0, bottom)
        at_layer(3, top)
        at_layer(1, second_layer)
        at_layer(2, third_layer)

    def line_5(g):
        def bottom():
            ag[g, "down", 1, 1].wait_recv()

        def top():
            ag[g, "up", 2, 2].wait_recv()

        def second_layer():
            ag[g, "up", 0, 0].wait_recv()
            ag[g, "up", 1, 0].start()

        def third_layer():
            ag[g, "down", 3, 3].wait_recv()
            ag[g, "down", 2, 3].start()

        at_layer(0, bottom)
        at_layer(3, top)
        at_layer(1, second_layer)
        at_layer(2, third_layer)

    def line_6(g):
        def bottom():
            ag[g, "down", 1, 2].wait_recv()

        def top():
            ag[g, "up", 2, 1].wait_recv()

        def second_layer():
            ag[g, "down", 2, 3].wait_recv()
            ag[g, "down", 1, 3].start()

        def third_layer():
            ag[g, "up", 1, 0].wait_recv()
            ag[g, "up", 2, 0].start()

        at_layer(0, bottom)
        at_layer(3, top)
        at_layer(1, second_layer)
        at_layer(2, third_layer)

    finals = {}

    def line_7(g):
        at_layer(0, lambda: ag[g, "down", 1, 3].wait_recv())
        at_layer(3, lambda: ag[g, "up", 2, 0].wait_recv())
        for side in range(2):
            here = pl.ds(pl.multiple_of(core * half + at(g, side), piece), piece)
            rows = full.at[g, pl.ds(side * piece, piece)]
            finals[g, side] = go(rows, bank.at[here], sibling)
            copy = fetch(rows, bank.at[here])
            copy.start()
            ends.append(copy)

    handed = []

    def results():
        def collect():
            for copy in taken:
                copy.wait()
            for copy in given:
                copy.wait_recv()
            size = mine.shape[1] // 8

            def add(i, _):
                rows = pl.ds(pl.multiple_of(i * size, size), size)
                for n in range(3):
                    add_rows(mine, (n, rows), (theirs, (n, rows)))
                return 0

            lax.fori_loop(0, 8, add, 0)
            score[...] = score[...] + scores[...]

        pl.when(holder)(collect)
        for rel in range(4):
            target = chips[rel]
            for n in range(4):
                out = (states_out, dx_out, dmem_out, halt_out)[n]
                share_ = out.shape[2]
                src = score if n == 3 else mine.at[n]
                src = src.at[:, pl.ds(pl.multiple_of(target * share_, share_), share_)]
                if rel == 0:
                    copy = fetch(src, out.at[s % 2])
                else:
                    copy = push(src, out.at[s % 2], across[rel - 1])
                pl.when(holder)(copy.start)
                handed.append((rel, copy))

    stages = [plane_first, plane_second, plane_third, line_1, line_2, line_3, line_4, line_5, line_6, line_7]
    lags = [0, 1, 2, 2, 3, 3, 4, 4, 5, 5]
    for tick in range(GROUPS + 6):
        for stage, lag in zip(stages, lags):
            if 0 <= tick - lag < GROUPS:
                stage(tick - lag)
        if tick <= len(gain_steps):
            gain_step(tick)
        if tick == RESULTS - 1:
            results_begin()
        if tick == RESULTS:
            results()

    for rel, copy in handed:
        if rel == 0:
            pl.when(holder)(copy.wait)
        else:
            pl.when(chips[rel] // 2 == core)(copy.wait_recv)
            pl.when(holder)(copy.wait_send)
    for copy in given:
        pl.when(jnp.logical_not(holder))(copy.wait_send)
    for copy in finals.values():
        copy.wait_recv()
    for copy in always:
        copy.wait_send()
    for copy in ends:
        copy.wait()
    for (g, way, z), copy in rs.items():
        at_layer(z, copy.wait_send)
    for (g, way, z, k), copy in ag.items():
        at_layer(z, copy.wait_send)


def reduce_all(dw, gains, states, dx, dmem, halt, sections):
    length, width = states.shape
    span = dw[0].shape[0]
    half = span // 2
    piece = half // 2 // GROUPS
    shares = width // sections
    micro = 2
    share = jax.ShapeDtypeStruct((micro, length, shares), bf16)
    outs = [jax.ShapeDtypeStruct((span, width), bf16), jax.ShapeDtypeStruct(gains.shape, f32), share, share, share,
            jax.ShapeDtypeStruct((micro, halt.shape[0], length // sections), f32)]
    copies = 8 * GROUPS + 4 + 5 + (4 + 2 + 6 + 12 + 2) * GROUPS + 12
    scratch = [
        pltpu.VMEM((4, half, width), bf16), pltpu.VMEM((4, half, width), bf16),
        pltpu.VMEM((GROUPS, 2, 2, piece, width), bf16), pltpu.VMEM((GROUPS, 2, piece, width), bf16),
        pltpu.VMEM((GROUPS, 2 * piece, width), bf16), pltpu.VMEM((GROUPS, 2 * piece, width), bf16),
        pltpu.VMEM((GROUPS, 2 * piece, width), bf16), pltpu.VMEM((GROUPS, 2 * piece, width), bf16),
        pltpu.VMEM((3, length, width), bf16), pltpu.VMEM((3, length, width), bf16),
        pltpu.VMEM(halt.shape, f32), pltpu.VMEM(halt.shape, f32),
        pltpu.VMEM((11,) + gains.shape, f32),
        pltpu.SemaphoreType.DMA((copies,)), pltpu.SemaphoreType.DMA((copies,)),
        pltpu.SemaphoreType.DMA((8 * GROUPS + 4 + 2 * GROUPS + 4,)),
    ]
    return pl.pallas_call(
        reduce_kernel,
        out_shape=outs,
        in_specs=[ANY] * 4 + [VMEM] + [ANY] * 4,
        out_specs=[ANY, VMEM, ANY, ANY, ANY, ANY],
        scratch_shapes=scratch,
        compiler_params=pltpu.CompilerParams(collective_id=1, has_side_effects=True, vmem_limit_bytes=52 * 2**20),
        name="reduce_all",
    )(*dw, gains, states, dx, dmem, halt)


def swap_cores(value):
    count = lax.axis_size("dp")
    return lax.ppermute(value, "dp", [(i, i ^ 1) for i in range(count)])


def gather_plain(states, memory, cotangent, bank, gains, ints):
    section, core = lax.axis_index("section"), lax.axis_index("dp") % 2
    micro = states.shape[0]
    holder = section // micro == core

    def pick(rows):
        own = lax.dynamic_index_in_dim(rows, section % micro, 0, keepdims=False)
        return jnp.where(holder, own, swap_cores(own))

    wide = [pick(lax.all_gather(t, "section", axis=2, tiled=True)) for t in (states, memory, cotangent)]
    return wide, lax.all_gather(bank, "section"), lax.all_gather(gains, "section"), [pick(t) for t in ints]


def reduce_plain(dw, dgains, states, dx, dmem, halt):
    section, core = lax.axis_index("section"), lax.axis_index("dp") % 2
    micro = 2
    holder = section // micro == core

    def to_shares(value):
        both = value.astype(f32) + swap_cores(value).astype(f32)
        both = jnp.where(holder, both, 0).astype(value.dtype)
        slots = jnp.stack([jnp.where(section % micro == i, both, 0) for i in range(micro)])
        return lax.psum_scatter(slots, "section", scatter_dimension=2, tiled=True)

    bank = lax.psum_scatter(jnp.stack(dw), "section", scatter_dimension=0, tiled=True)[0]
    bank = lax.psum(bank.astype(f32), "dp")
    gain_sum = lax.psum_scatter(jnp.stack(dgains), "section", scatter_dimension=0, tiled=True)[0]
    gain_sum = lax.psum(gain_sum, "dp")
    return bank, gain_sum, *[to_shares(t) for t in (states, dx, dmem, halt)]


def local(
    states_in, memory, cotangent, weight_bank, gain_bank, segments, pad_mask, memory_segments, memory_mask, exit_depths
):
    section, sections = lax.axis_index("section"), lax.axis_size("section")
    core = lax.axis_index("dp") % 2
    matrices = weight_bank.shape[1:]
    width = matrices[-1]
    ints = (segments, pad_mask, memory_segments, memory_mask, exit_depths)
    near = sections == 4 and lax.axis_size("dp") == 8
    if near:
        x, mem, top, bank, gains, *ints = gather_all(
            states_in, memory, cotangent, weight_bank[0].reshape(-1, width), gain_bank[0], ints
        )
        bank = bank.reshape((sections,) + matrices)
        ints, row = [t.reshape(-1, t.shape[-1]) for t in ints], section
    else:
        (x, mem, top), bank, gains, ints = gather_plain(
            states_in, memory, cotangent, weight_bank[0], gain_bank[0], ints
        )
        ints, row = [t[None] for t in ints], jnp.zeros((), i32)
    states, halt, dx, dmem, dw, dgains = row_forward_backward(
        row, core, x, mem, top, bank, [gains[i] for i in range(sections)], ints
    )
    if near:
        grads = [t.reshape(-1, width) for t in dw]
        bank, gain_sum, states, dx, dmem, halt = reduce_all(
            grads, jnp.concatenate(dgains), states, dx, dmem, halt, sections
        )
        bank = bank.reshape(matrices)
        gain_sum = lax.dynamic_index_in_dim(gain_sum.reshape(sections, 2, width), section, 0, keepdims=False)
    else:
        bank, gain_sum, states, dx, dmem, halt = reduce_plain(dw, dgains, states, dx, dmem, halt)
    return (
        states,
        halt[:, :2],
        dx.astype(f32),
        dmem.astype(f32),
        bank.astype(f32)[None],
        gain_sum[None],
    )


def solution(mesh):
    rows = P("dp", None, "section")
    return jax.shard_map(
        local,
        mesh=mesh,
        in_specs=(
            rows, rows, rows, P("section", None, None, None), P("section", None, None),
            P("dp", None), P("dp", None), P("dp", None), P("dp", None), P("dp", None),
        ),
        out_specs=(rows, rows, rows, rows, P("section", None, None, None), P("section", None, None)),
        check_vma=False,
    )
```

profile of v0, /device:TPU:0, one launch (start us, length us, event | category | flops | bytes accessed | tf_op | source)
XLA Modules:
  0.0 439.1 jit_solution(12836890001788163437)
XLA Ops:
  0.7 2.2 copy-done.1
  2.8 1.0 copy-done.2
  3.9 1.0 copy-done.3
  4.9 1.0 copy-done.4
  6.0 0.7 copy-done.6
  6.7 0.7 copy-done.7
  7.4 0.7 copy-done.8
  8.1 0.7 copy-done.9
  8.8 0.7 copy-done.10
  9.4 0.7 copy-done.12
  10.1 75.5 %gather_all.1 = (bf16[1024,512]{1,0:T(8,128)(2,1)S(1)}, bf16[1024,512]{1,0:T(8,128)(2,1)S(1)}, bf16[1024,512]{1,0:T(8,128)(2,1)S(1)}, bf16[16384,512]{1,0:T(8,12...) custom-call(bf16[2,1024,128]{2,1,0:T(8,128)(2,1)S(1)} %copy-done.2, ...), custom_call_target="tpu_custom_call" | custom-call | tf_op jit(solution)/shard_map/gather_all/pallas_call | solution.py:949
  85.7 5.7 %copy-done = bf16[16384,512]{1,0:T(8,128)(2,1)} copy-done((bf16[16384,512]{1,0:T(8,128)(2,1)}, bf16[16384,512]{1,0:T(8,128)(2,1)S(1)}, u32[]{:S(2)}) %copy-start) | copy-done | bytes 16777240
  92.0 1.0 copy-done.13
  93.0 1.0 copy-done.14
  93.9 1.0 copy-done.15
  94.9 0.6 reshape.58.seg
  95.5 0.6 reshape.59.pad
  96.8 0.6 reshape.61.mmask
  98.0 2.0 make_plan.1
  100.0 25.5 %attend_zero.1 = (bf16[1024,1536]{1,0:T(8,128)(2,1)}, bf16[1024,512]{1,0:T(8,128)(2,1)}, f32[8,1024]{1,0:T(8,128)}, f32[1024,512]{1,0:T(8,128)}, bf16[1024,512]{...) custom-call(s32[8,128]{1,0:T(8,128)} %get-tuple-element.68.meta, ...), custom_call_target="tpu_custom_call" | custom-call | flops 6000000000 | bytes 20971520 | tf_op jit(solution)/shard_map/attend_zero/pallas_call | solution.py:662
  125.5 10.1 %dense_one.1 = (bf16[1024,512]{1,0:T(8,128)(2,1)}, f32[8,1024]{1,0:T(8,128)}, f32[1,512]{1,0:T(1,128)}) custom-call(s32[8,128]{1,0:T(8,128)} %get-tuple-element.68.meta, bf16[4,8,512,512]{3,2,1,0:T(8,128)(2,1)} %bitcast.21, bf16[1024,512]{1,0:T(8,128)(2,1)} %get-tuple-element.83.x, f32[2,512]{1,0:T(2,128)} %get-tuple-element.122.gain, ...), custom_call_target="tpu_custom_call" | custom-call | flops 4000000000 | bytes 20971520 | tf_op jit(solution)/shard_map/dense_one/pallas_call | solution.py:662
  135.6 23.2 %attend_two.1 = (bf16[1024,1536]{1,0:T(8,128)(2,1)}, bf16[1024,512]{1,0:T(8,128)(2,1)}, f32[8,1024]{1,0:T(8,128)}, f32[1024,512]{1,0:T(8,128)}, bf16[1024,512]{1...) custom-call(s32[8,128]{1,0:T(8,128)} %get-tuple-element.68.meta, ...), custom_call_target="tpu_custom_call" | custom-call | flops 6000000000 | bytes 20971520 | tf_op jit(solution)/shard_map/attend_two/pallas_call | solution.py:662
  158.8 20.4 %dense_three.1 = (bf16[1024,512]{1,0:T(8,128)(2,1)}, bf16[8,512,512]{2,1,0:T(8,128)(2,1)}, f32[2,512]{1,0:T(2,128)}, bf16[1024,512]{1,0:T(8,128)(2,1)}, f32[8,1024]{1,0:T(8,128)}) custom-call(s32[8,128]{1,0:T(8,128)} %get-tuple-element.68.meta, bf16[4,8,512,512]{3,2,1,0:T(8,128)(2,1)} %bitcast.23, bf16[1024,512]{1,0:T(8,128)(2,1)} %get-tuple-element.94.x, ...), custom_call_target="tpu_custom_call" | custom-call | flops 8000000000 | bytes 20971520 | tf_op jit(solution)/shard_map/dense_three/pallas_call | solution.py:662
  179.2 29.8 %attend_two_back.1 = (bf16[1024,512]{1,0:T(8,128)(2,1)}, bf16[1024,512]{1,0:T(8,128)(2,1)}, bf16[8,512,512]{2,1,0:T(8,128)(2,1)}, f32[2,512]{1,0:T(2,128)}) custom-call(s32[8,128]{1,0:T(8,128)} %get-tuple-element.68.meta, bf16[4,8,512,512]{3,2,1,0:T(8,128)(2,1)} %bitcast.24, bf16[1024,512]{1,0:T(8,128)(2,1)} %get-tuple-element.85.x_in, ...), custom_call_target="tpu_custom_call" | custom-call | flops 12000000000 | bytes 20971520 | tf_op jit(solution)/shard_map/attend_two_back/pallas_call | solution.py:662
  208.9 17.1 %dense_one_back.1 = (bf16[1024,512]{1,0:T(8,128)(2,1)}, bf16[8,512,512]{2,1,0:T(8,128)(2,1)}, f32[2,512]{1,0:T(2,128)}) custom-call(s32[8,128]{1,0:T(8,128)} %get-tuple-element.68.meta, bf16[4,8,512,512]{3,2,1,0:T(8,128)(2,1)} %bitcast.25, bf16[1024,512]{1,0:T(8,128)(2,1)} %get-tuple-element.83.x, f32[2,512]{1,0:T(2,128)} %get-tuple-element.122.gain, ...), custom_call_target="tpu_custom_call" | custom-call | flops 8000000000 | bytes 20971520 | tf_op jit(solution)/shard_map/dense_one_back/pallas_call | solution.py:662
  226.1 32.2 %attend_zero_back.1 = (bf16[1024,512]{1,0:T(8,128)(2,1)}, bf16[1024,512]{1,0:T(8,128)(2,1)}, bf16[8,512,512]{2,1,0:T(8,128)(2,1)}, f32[2,512]{1,0:T(2,128)}) custom-call(s32[8,128]{1,0:T(8,128)} %get-tuple-element.68.meta, bf16[4,8,512,512]{3,2,1,0:T(8,128)(2,1)} %bitcast.26, bf16[1024,512]{1,0:T(8,128)(2,1)} %copy-done.13, bf16[1024,512]{1,0:T(8,128)(2,1)} %copy-done.14, ...), custom_call_target="tpu_custom_call" | custom-call | flops 12000000000 | bytes 20971520 | tf_op jit(solution)/shard_map/attend_zero_back/pallas_call | solution.py:662
  258.3 0.7 pad_maximum_fusion.gains
  259.1 168.7 %reduce_all.1 = (bf16[4096,512]{1,0:T(8,128)(2,1)}, f32[8,512]{1,0:T(8,128)S(1)}, bf16[2,1024,128]{2,1,0:T(8,128)(2,1)S(1)}, bf16[2,1024,128]{2,1,0:T(8,128)(2,1...) custom-call(bf16[4096,512]{1,0:T(8,128)(2,1)} %bitcast.34, bf16[4096,512]{1,0:T(8,128)(2,1)} %bitcast.33, ...), custom_call_target="tpu_custom_call" | custom-call | tf_op jit(solution)/shard_map/reduce_all/pallas_call | solution.py:1323
  429.0 1.0 convert_element_type.19
  430.0 1.0 convert_element_type.20
  431.1 6.7 %convert.1 = f32[1,8,512,512]{3,2,1,0:T(8,128)} convert(bf16[1,8,512,512]{3,2,1,0:T(8,128)(2,1)} %bitcast.30) | non-fusion elementwise | flops 2097152 | bytes 12582912 | tf_op jit(solution)/shard_map/convert_element_type | solution.py:1407
  437.8 0.8 copy.17
  (29 shorter events, 3.1 us)
Async XLA Ops:
  0.6 2.2 copy-start.1
  2.8 1.0 copy-start.2
  3.9 1.0 copy-start.3
  4.9 1.0 copy-start.4
  6.0 0.7 copy-start.6
  6.7 0.7 copy-start.7
  7.4 0.7 copy-start.8
  8.1 0.7 copy-start.9
  8.8 0.7 copy-start.10
  9.4 0.7 copy-start.12
  85.7 5.7 %copy-start = (bf16[16384,512]{1,0:T(8,128)(2,1)}, bf16[16384,512]{1,0:T(8,128)(2,1)S(1)}, u32[]{:S(2)}) copy-start(bf16[16384,512]{1,0:T(8,128)(2,1)S(1)} %get-tuple-element.69) | copy-start | bytes 50331652
  91.4 0.6 copy-start.11
  92.0 1.0 copy-start.13
  93.0 1.0 copy-start.14
  93.9 1.0 copy-start.15
  226.0 32.3 %copy-start.16 = (f32[2,512]{1,0:T(2,128)S(1)}, f32[2,512]{1,0:T(2,128)}, u32[]{:S(2)}) copy-start(f32[2,512]{1,0:T(2,128)} %get-tuple-element.109) | copy-start | bytes 12292
  226.1 32.3 %copy-start.17 = (f32[2,512]{1,0:T(2,128)S(1)}, f32[2,512]{1,0:T(2,128)}, u32[]{:S(2)}) copy-start(f32[2,512]{1,0:T(2,128)} %get-tuple-element.108) | copy-start | bytes 12292
  226.1 32.3 %copy-start.18 = (f32[2,512]{1,0:T(2,128)S(1)}, f32[2,512]{1,0:T(2,128)}, u32[]{:S(2)}) copy-start(f32[2,512]{1,0:T(2,128)} %get-tuple-element.107) | copy-start | bytes 12292
  226.1 33.0 %copy-start.5 = (f32[8,1024]{1,0:T(8,128)S(1)}, f32[8,1024]{1,0:T(8,128)}, u32[]{:S(2)}) copy-start(f32[8,1024]{1,0:T(8,128)} %get-tuple-element.113.halt) | copy-start | bytes 98308
where the time goes:
time: 443 us; the launch traced here: 439 us
  Pallas kernels  404 us (91%)
  local copies, waits for them, and re-layouts  23.8 us (5%)
  other arithmetic  9.52 us (2%)
    pallas_call x1, Pallas kernels, reduce_all(): pl.pallas_call(reduce_kernel, out_shape=outs, in_specs=[ANY] * 4 + [VMEM]...  169 us
    pallas_call x7, Pallas kernels, run(): pl.pallas_call(kernel, out_shape=[jax.ShapeDtypeStruct(shape, dtype) for...  158 us
    pallas_call x1, Pallas kernels, gather_all(): pl.pallas_call(gather_kernel, out_shape=outs, in_specs=[ANY] * 10, out_sp...  75.5 us
    unnamed x39, local copies, waits for them, and re-layouts  19.5 us

commit v1 on v0

--- a/solution.py
+++ b/solution.py
@@ -174,19 +174,25 @@
 
             def one_window(n, _):
                 keys, bias = key_window(meta, kind, top, i, n, low, high)
+                scores = [dot_nt(k[keys, lanes_of(k_at, p)], both_q[p]) for p in range(pairs)]
+                weights, fades = [], []
                 for p in range(pairs):
-                    scores = dot_nt(k[keys, lanes_of(k_at, p)], both_q[p]) + bias
+                    tile = scores[p] + bias
                     before = peaks[p : p + 1, :]
-                    peak = jnp.maximum(before, jnp.max(scores, axis=0, keepdims=True))
+                    peak = jnp.maximum(before, jnp.max(tile, axis=0, keepdims=True))
                     fade = jnp.exp(before - peak)
-                    weights = jnp.exp(scores - peak)
+                    weight = jnp.exp(tile - peak)
                     peaks[p : p + 1, :] = peak
-                    totals[p : p + 1, :] = totals[p : p + 1, :] * fade + jnp.sum(weights, axis=0, keepdims=True)
-                    mixed = both_blocks(dot_tn(v[keys, lanes_of(v_at, p)], weights.astype(bf16)))
+                    totals[p : p + 1, :] = totals[p : p + 1, :] * fade + jnp.sum(weight, axis=0, keepdims=True)
+                    weights.append(weight.astype(bf16))
+                    fades.append(fade)
+                mixes = [dot_tn(v[keys, lanes_of(v_at, p)], weights[p]) for p in range(pairs)]
+                for p in range(pairs):
+                    fade = fades[p]
                     faded = jnp.concatenate(
                         [jnp.broadcast_to(fade[:, :BLOCK], (64, BLOCK)), jnp.broadcast_to(fade[:, BLOCK:], (64, BLOCK))]
                     )
-                    sums[p] = sums[p] * faded + mixed
+                    sums[p] = sums[p] * faded + both_blocks(mixes[p])
                 return 0
 
             lax.fori_loop(0, count, one_window, 0)
@@ -225,16 +231,20 @@
 
             def one_window(n, _):
                 keys, bias = key_window(meta, kind, top, i, n, low, high)
+                these = [k[keys, lanes_of(k_at, p)] for p in range(pairs)]
+                scores = [dot_nt(these[p], both_q[p]) for p in range(pairs)]
+                grad_probs = [dot_nt(v[keys, lanes_of(v_at, p)], both_o[p]) for p in range(pairs)]
+                probs = [jnp.exp(scores[p] + bias - two_rows(lse, p, rows)) for p in range(pairs)]
+                grad_scores = [
+                    (probs[p] * (grad_probs[p] - two_rows(delta, p, rows))).astype(bf16) for p in range(pairs)
+                ]
+                grads_v = [dot(probs[p].astype(bf16), both_o[p]) for p in range(pairs)]
+                grads_k = [dot(grad_scores[p], both_q[p]) for p in range(pairs)]
+                grads_q = [dot_tn(these[p], grad_scores[p]) for p in range(pairs)]
                 for p in range(pairs):
-                    lanes = lanes_of(0, p)
-                    these = k[keys, lanes_of(k_at, p)]
-                    queries, grads = both_q[p], both_o[p]
-                    probs = jnp.exp(dot_nt(these, queries) + bias - two_rows(lse, p, rows))
-                    grad_probs = dot_nt(v[keys, lanes_of(v_at, p)], grads)
-                    grad_scores = (probs * (grad_probs - two_rows(delta, p, rows))).astype(bf16)
-                    dv[keys, lanes] += dot(probs.astype(bf16), grads)
-                    dk[keys, lanes] += dot(grad_scores, queries)
-                    sums[p] += both_blocks(dot_tn(these, grad_scores))
+                    dv[keys, lanes_of(0, p)] += grads_v[p]
+                    dk[keys, lanes_of(0, p)] += grads_k[p]
+                    sums[p] += both_blocks(grads_q[p])
                 return 0
 
             lax.fori_loop(0, count, one_window, 0)
@@ -586,10 +596,30 @@
     depth = of_token(depth_table)
     keep = depth == 2
 
-    later = lax.broadcasted_iota(i32, (sentences, 1), 0) > 0
-    away = jnp.where(later, jnp.abs(starts - length // 2), length)
-    nearest = jnp.min(away, axis=0, keepdims=True)
-    cut = jnp.min(jnp.where(away == nearest, starts, length), axis=0, keepdims=True)
+    def by_block(values):
+        return jnp.concatenate([values[:, i * BLOCK : (i + 1) * BLOCK] for i in range(blocks)], axis=0)
+
+    def spans(used, lows, highs):
+        lows = jnp.min(by_block(jnp.where(used, lows, slots)), axis=1, keepdims=True)
+        highs = jnp.max(by_block(jnp.where(used, highs, 0)), axis=1, keepdims=True)
+        return jnp.minimum(lows, highs) // STEP * STEP, highs
+
+    work = jnp.zeros((blocks, 1), i32)
+    for used in (place >= 0, keep):
+        for lows, highs in ((low, high), (cross_low, cross_high)):
+            from_, to = spans(used, lows, highs)
+            work = work + 2 * ((to - from_ + KEYS - 1) // KEYS) + jnp.where(to > from_, 1, 0)
+    start = jnp.sum(jnp.where(square, starts, 0), axis=0, keepdims=True)
+    block_at = lax.broadcasted_iota(i32, (blocks, sentences), 0) * BLOCK
+    before = jnp.sum(jnp.where(block_at < start, work, 0), axis=0, keepdims=True)
+    after = jnp.sum(jnp.where(block_at + BLOCK > start, work, 0), axis=0, keepdims=True)
+    after = after + jnp.where(filled < length, 5, 0)
+    off = jnp.abs(start - length // 2)
+    score = jnp.maximum(before, after) * length + off
+    score = score + jnp.where(off > length // 8, length * length, 0)
+    score = jnp.where(lax.broadcasted_iota(i32, (1, sentences), 1) > 0, score, 2 * length * length)
+    best = jnp.min(score, axis=1, keepdims=True)
+    cut = jnp.min(jnp.where(score == best, start, length), axis=1, keepdims=True)
 
     def by_core(first, second):
         return first * (1 - core) + second * core
@@ -606,9 +636,6 @@
 
     def top_of(flag):
         return jnp.where(flag == 1, length - KEYS, base + wide - KEYS)
-
-    def by_block(values):
-        return jnp.concatenate([values[:, i * BLOCK : (i + 1) * BLOCK] for i in range(blocks)], axis=0)
 
     lane = lax.broadcasted_iota(i32, (blocks, 128), 1)
     table = jnp.zeros((blocks, 128), i32)
@@ -617,10 +644,7 @@
     for layer in range(2):
         used = owned if layer == 0 else owned & keep
         for kind, lows, highs in ((SELF, low, high), (CROSS, cross_low, cross_high)):
-            lows = jnp.min(by_block(jnp.where(used, lows, slots)), axis=1, keepdims=True)
-            highs = jnp.max(by_block(jnp.where(used, highs, 0)), axis=1, keepdims=True)
-            entries[kind + 4 * layer] = jnp.minimum(lows, highs) // STEP * STEP
-            entries[kind + 4 * layer + 1] = highs
+            entries[kind + 4 * layer], entries[kind + 4 * layer + 1] = spans(used, lows, highs)
         flag_m = outside(
             jnp.min(jnp.where(used, cross_low, slots), axis=1, keepdims=True),
             jnp.max(jnp.where(used, cross_high, 0), axis=1, keepdims=True),
@@ -640,7 +664,7 @@
         cols[i * BLOCK : (i + 1) * BLOCK, :] = by_row[:, i * BLOCK : (i + 1) * BLOCK].T
 
 
-ANY = pl.BlockSpec(memory_space=pl.ANY)
+ANY = pl.BlockSpec(memory_space=pltpu.HBM)
 VMEM = pl.BlockSpec(memory_space=pltpu.VMEM)
 SMEM = pl.BlockSpec(memory_space=pltpu.SMEM)
 
@@ -654,6 +678,7 @@
         out_shape=[jax.ShapeDtypeStruct(*out) for out in outs],
         in_specs=[SMEM, SMEM] + [VMEM] * 5,
         out_specs=[VMEM] * 4,
+        compiler_params=pltpu.CompilerParams(vmem_limit_bytes=60 * 2**20),
         name="make_plan",
     )(row.astype(i32)[None], core.astype(i32)[None], seg, pad, mseg, mmask, depths)
 
@@ -953,7 +978,7 @@
         out_specs=[ANY] * 10,
         scratch_shapes=[pltpu.VMEM(bank.shape, bank.dtype), pltpu.SemaphoreType.DMA((copies,)), pltpu.SemaphoreType.DMA((copies,)),
                         pltpu.SemaphoreType.DMA((12,))],
-        compiler_params=pltpu.CompilerParams(collective_id=0, has_side_effects=True, vmem_limit_bytes=16 * 2**20),
+        compiler_params=pltpu.CompilerParams(collective_id=0, has_side_effects=True, vmem_limit_bytes=60 * 2**20),
         name="gather_all",
     )(states, memory, cotangent, bank, gains, *ints)
 

time: 443 us -> 392 us (0.88)
  the two profiles are of different devices: /device:TPU:0 before, /device:TPU:5 now
where the time goes in v1:
time: 392 us; the launch traced here: 385 us
  Pallas kernels  365 us (93%)
  other arithmetic  9.52 us (2%)
  local copies, waits for them, and re-layouts  8.68 us (2%)
    pallas_call x1, Pallas kernels, reduce_all(): pl.pallas_call(reduce_kernel, out_shape=outs, in_specs=[ANY] * 4 + [VMEM]...  148 us
    pallas_call x7, Pallas kernels, run(): pl.pallas_call(kernel, out_shape=[jax.ShapeDtypeStruct(shape, dtype) for...  139 us
    pallas_call x1, Pallas kernels, gather_all(): pl.pallas_call(gather_kernel, out_shape=outs, in_specs=[ANY] * 10, out_sp...  75.5 us

profile of v1, /device:TPU:5, one launch (start us, length us, event | category | flops | bytes accessed | tf_op | source)
XLA Modules:
  0.0 384.6 jit_solution(9411469845159759302)
XLA Ops:
  0.6 75.5 %gather_all.1 = (bf16[1024,512]{1,0:T(8,128)(2,1)}, bf16[1024,512]{1,0:T(8,128)(2,1)}, bf16[1024,512]{1,0:T(8,128)(2,1)}, bf16[16384,512]{1,0:T(8,128)(2,1)}, f3...) custom-call(bf16[2,1024,128]{2,1,0:T(8,128)(2,1)} %states.1, ...), custom_call_target="tpu_custom_call" | custom-call | tf_op jit(solution)/shard_map/gather_all/pallas_call | solution.py:974
  76.2 1.3 reshape.58.seg
  77.5 1.3 reshape.59.pad
  78.8 1.3 reshape.60.mseg
  80.2 1.3 reshape.61.mmask
  81.5 1.3 slice_bitcast_fusion
  82.8 2.5 make_plan.1
  85.3 18.1 %attend_zero.1 = (bf16[1024,1536]{1,0:T(8,128)(2,1)}, bf16[1024,512]{1,0:T(8,128)(2,1)}, f32[8,1024]{1,0:T(8,128)}, f32[1024,512]{1,0:T(8,128)}, bf16[1024,512]{...) custom-call(s32[8,128]{1,0:T(8,128)} %get-tuple-element.68.meta, ...), custom_call_target="tpu_custom_call" | custom-call | flops 6000000000 | bytes 20971520 | tf_op jit(solution)/shard_map/attend_zero/pallas_call | solution.py:687
  103.4 10.1 %dense_one.1 = (bf16[1024,512]{1,0:T(8,128)(2,1)}, f32[8,1024]{1,0:T(8,128)}, f32[1,512]{1,0:T(1,128)}) custom-call(s32[8,128]{1,0:T(8,128)} %get-tuple-element.68.meta, bf16[4,8,512,512]{3,2,1,0:T(8,128)(2,1)} %bitcast.21, bf16[1024,512]{1,0:T(8,128)(2,1)} %get-tuple-element.83.x, f32[2,512]{1,0:T(2,128)} %get-tuple-element.122.gain, ...), custom_call_target="tpu_custom_call" | custom-call | flops 4000000000 | bytes 20971520 | tf_op jit(solution)/shard_map/dense_one/pallas_call | solution.py:687
  113.5 16.6 %attend_two.1 = (bf16[1024,1536]{1,0:T(8,128)(2,1)}, bf16[1024,512]{1,0:T(8,128)(2,1)}, f32[8,1024]{1,0:T(8,128)}, f32[1024,512]{1,0:T(8,128)}, bf16[1024,512]{1...) custom-call(s32[8,128]{1,0:T(8,128)} %get-tuple-element.68.meta, ...), custom_call_target="tpu_custom_call" | custom-call | flops 6000000000 | bytes 20971520 | tf_op jit(solution)/shard_map/attend_two/pallas_call | solution.py:687
  130.1 20.4 %dense_three.1 = (bf16[1024,512]{1,0:T(8,128)(2,1)}, bf16[8,512,512]{2,1,0:T(8,128)(2,1)}, f32[2,512]{1,0:T(2,128)}, bf16[1024,512]{1,0:T(8,128)(2,1)}, f32[8,1024]{1,0:T(8,128)}) custom-call(s32[8,128]{1,0:T(8,128)} %get-tuple-element.68.meta, bf16[4,8,512,512]{3,2,1,0:T(8,128)(2,1)} %bitcast.23, bf16[1024,512]{1,0:T(8,128)(2,1)} %get-tuple-element.94.x, ...), custom_call_target="tpu_custom_call" | custom-call | flops 8000000000 | bytes 20971520 | tf_op jit(solution)/shard_map/dense_three/pallas_call | solution.py:687
  150.5 27.3 %attend_two_back.1 = (bf16[1024,512]{1,0:T(8,128)(2,1)}, bf16[1024,512]{1,0:T(8,128)(2,1)}, bf16[8,512,512]{2,1,0:T(8,128)(2,1)}, f32[2,512]{1,0:T(2,128)}) custom-call(s32[8,128]{1,0:T(8,128)} %get-tuple-element.68.meta, bf16[4,8,512,512]{3,2,1,0:T(8,128)(2,1)} %bitcast.24, bf16[1024,512]{1,0:T(8,128)(2,1)} %get-tuple-element.85.x_in, ...), custom_call_target="tpu_custom_call" | custom-call | flops 12000000000 | bytes 20971520 | tf_op jit(solution)/shard_map/attend_two_back/pallas_call | solution.py:687
  177.8 17.1 %dense_one_back.1 = (bf16[1024,512]{1,0:T(8,128)(2,1)}, bf16[8,512,512]{2,1,0:T(8,128)(2,1)}, f32[2,512]{1,0:T(2,128)}) custom-call(s32[8,128]{1,0:T(8,128)} %get-tuple-element.68.meta, bf16[4,8,512,512]{3,2,1,0:T(8,128)(2,1)} %bitcast.25, bf16[1024,512]{1,0:T(8,128)(2,1)} %get-tuple-element.83.x, f32[2,512]{1,0:T(2,128)} %get-tuple-element.122.gain, ...), custom_call_target="tpu_custom_call" | custom-call | flops 8000000000 | bytes 20971520 | tf_op jit(solution)/shard_map/dense_one_back/pallas_call | solution.py:687
  194.9 0.0 copy-start.1
  194.9 0.0 copy-start.2
  194.9 0.0 copy-start.3
  194.9 0.0 copy-start
  195.0 29.8 %attend_zero_back.1 = (bf16[1024,512]{1,0:T(8,128)(2,1)}, bf16[1024,512]{1,0:T(8,128)(2,1)}, bf16[8,512,512]{2,1,0:T(8,128)(2,1)}, f32[2,512]{1,0:T(2,128)}) custom-call(s32[8,128]{1,0:T(8,128)} %get-tuple-element.68.meta, bf16[4,8,512,512]{3,2,1,0:T(8,128)(2,1)} %bitcast.26, bf16[1024,512]{1,0:T(8,128)(2,1)} %get-tuple-element.70.x_in, ...), custom_call_target="tpu_custom_call" | custom-call | flops 12000000000 | bytes 20971520 | tf_op jit(solution)/shard_map/attend_zero_back/pallas_call | solution.py:687
  224.8 0.0 copy-done.1
  224.8 0.0 copy-done.2
  224.8 0.0 copy-done.3
  224.8 0.7 pad_maximum_fusion.gains
  225.5 0.0 copy-done
  225.5 147.8 %reduce_all.1 = (bf16[4096,512]{1,0:T(8,128)(2,1)}, f32[8,512]{1,0:T(8,128)S(1)}, bf16[2,1024,128]{2,1,0:T(8,128)(2,1)S(1)}, bf16[2,1024,128]{2,1,0:T(8,128)(2,1...) custom-call(bf16[4096,512]{1,0:T(8,128)(2,1)} %bitcast.32, bf16[4096,512]{1,0:T(8,128)(2,1)} %bitcast.31, ...), custom_call_target="tpu_custom_call" | custom-call | tf_op jit(solution)/shard_map/reduce_all/pallas_call | solution.py:1348
  373.4 0.6 slice.19
  374.0 0.6 constant_dynamic-slice_fusion
  374.6 1.0 convert_element_type.19
  375.6 1.0 convert_element_type.20
  376.6 6.7 %convert.1 = f32[1,8,512,512]{3,2,1,0:T(8,128)} convert(bf16[1,8,512,512]{3,2,1,0:T(8,128)(2,1)} %bitcast.27) | non-fusion elementwise | flops 2097152 | bytes 12582912 | tf_op jit(solution)/shard_map/convert_element_type | solution.py:1432
  383.4 0.8 copy.17
  (1 shorter events, 0.0 us)
Async XLA Ops:
  194.9 29.9 %copy-start.1 = (f32[2,512]{1,0:T(2,128)S(1)}, f32[2,512]{1,0:T(2,128)}, u32[]{:S(2)}) copy-start(f32[2,512]{1,0:T(2,128)} %get-tuple-element.109) | copy-start | bytes 12292
  194.9 29.9 %copy-start.2 = (f32[2,512]{1,0:T(2,128)S(1)}, f32[2,512]{1,0:T(2,128)}, u32[]{:S(2)}) copy-start(f32[2,512]{1,0:T(2,128)} %get-tuple-element.108) | copy-start | bytes 12292
  194.9 29.9 %copy-start.3 = (f32[2,512]{1,0:T(2,128)S(1)}, f32[2,512]{1,0:T(2,128)}, u32[]{:S(2)}) copy-start(f32[2,512]{1,0:T(2,128)} %get-tuple-element.107) | copy-start | bytes 12292
  194.9 30.6 %copy-start = (f32[8,1024]{1,0:T(8,128)S(1)}, f32[8,1024]{1,0:T(8,128)}, u32[]{:S(2)}) copy-start(f32[8,1024]{1,0:T(8,128)} %get-tuple-element.113.halt) | copy-start | bytes 98308

commit v2 on v1

--- a/solution.py
+++ b/solution.py
@@ -35,16 +35,6 @@
     return lax.dot_general(left, right, (((0,), (0,)), ((), ())), preferred_element_type=f32)
 
 
-def exact_nt(left, right):
-    return lax.dot_general(
-        left, right, (((1,), (1,)), ((), ())), precision=lax.Precision.HIGHEST, preferred_element_type=f32
-    )
-
-
-def exact(left, right):
-    return jnp.dot(left, right, precision=lax.Precision.HIGHEST, preferred_element_type=f32)
-
-
 def norm(x, gain):
     return x * lax.rsqrt(jnp.mean(x * x, axis=-1, keepdims=True) + EPS) * gain
 
@@ -61,16 +51,12 @@
 GELU_B = 0.044715
 
 
-def gelu(z):
-    return 0.5 * z * (1.0 + jnp.tanh(GELU_A * (z + GELU_B * z * z * z)))
-
-
 def gelu_both(z):
     square = z * z
-    bend = jnp.tanh(GELU_A * z * (1.0 + GELU_B * square))
-    half = 0.5 * (1.0 + bend)
-    slope = half + 0.5 * z * (1.0 - bend * bend) * (GELU_A * (1.0 + 3.0 * GELU_B * square))
-    return z * half, slope
+    bend = jnp.tanh(z * (GELU_A + GELU_A * GELU_B * square))
+    half = 0.5 * bend + 0.5
+    value = z * half
+    return value, half + value * (1.0 - bend) * (GELU_A + 3.0 * GELU_A * GELU_B * square)
 
 
 def windows(meta, length):
@@ -276,7 +262,7 @@
         wait()
 
     def self_in(rows, _):
-        a = norm(x[rows, :].astype(f32), gain[0:1, :]).astype(bf16)
+        a = norm(x[rows, :].astype(f32), gain[section, 0:1]).astype(bf16)
         both = dot(a, wide[...])
         qkv[rows, :width] = (both[:, :width] * 0.125).astype(bf16)
         qkv[rows, width:] = both[:, width:].astype(bf16)
@@ -307,7 +293,7 @@
     def cross_in(rows, _):
         state = x[rows, :].astype(f32) + go(rows) * dot(o1[rows, :], third[...])
         mid[rows, :] = state
-        a = norm(state, gain[1:2, :]).astype(bf16)
+        a = norm(state, gain[section, 1:2]).astype(bf16)
         q2[rows, :] = (dot(a, fourth[...]) * 0.125).astype(bf16)
 
     over(meta, FLAG_T, length, cross_in)
@@ -420,13 +406,13 @@
     weight_grad([5, 6], flag_m, lambda rows: mem[rows, :], lambda rows: dqkv[rows, width:])
 
     def cross_out(rows, fresh):
-        grad_x, grad_gain = norm_back(mid[rows, :], gain[1:2, :], dot_nt(dqkv[rows, :width], fourth[...]))
+        grad_x, grad_gain = norm_back(mid[rows, :], gain[section, 1:2], dot_nt(dqkv[rows, :width], fourth[...]))
         dstate[rows, :] = top_grad(rows) + grad_x
         dgain[1:2, :] = grad_gain if fresh else dgain[1:2, :] + grad_gain
 
     over(meta, FLAG_T, length, cross_out)
     weight_grad(
-        [4], FLAG_T, lambda rows: norm(mid[rows, :], gain[1:2, :]).astype(bf16), lambda rows: dqkv[rows, :width]
+        [4], FLAG_T, lambda rows: norm(mid[rows, :], gain[section, 1:2]).astype(bf16), lambda rows: dqkv[rows, :width]
     )
     for wait in third_here:
         wait()
@@ -443,7 +429,7 @@
     def self_out(rows, fresh):
         dqkv[rows, width : 2 * width] = dk[rows, :].astype(bf16)
         dqkv[rows, 2 * width :] = dv[rows, :].astype(bf16)
-        grad_x, grad_gain = norm_back(x[rows, :].astype(f32), gain[0:1, :], dot_nt(dqkv[rows, :], wide[...]))
+        grad_x, grad_gain = norm_back(x[rows, :].astype(f32), gain[section, 0:1], dot_nt(dqkv[rows, :], wide[...]))
         value = dstate[rows, :] + grad_x
         if entry:
             value = jnp.where(go_rows[rows, 2:3] > 0.0, value, 0.0)
@@ -456,19 +442,19 @@
     else:
         moves.away(dx, dx_out, FLAG_T)
     weight_grad(
-        [0, 1, 2], FLAG_T, lambda rows: norm(x[rows, :].astype(f32), gain[0:1, :]).astype(bf16),
+        [0, 1, 2], FLAG_T, lambda rows: norm(x[rows, :].astype(f32), gain[section, 0:1]).astype(bf16),
         lambda rows: dqkv[rows, :],
     )
     moves.finish()
 
 
-def exit_part(layer, vector, frows, rows, target_row, halt, exit_grad, fresh, sentences):
+def exit_part(layer, vector, cols, rows, last, score_at, exit_grad, fresh, sentences):
     factor = layer.shape[1] ** (-0.5)
-    vectors = jnp.broadcast_to(vector, (8, layer.shape[1]))
-    score = jax.nn.sigmoid(exact_nt(vectors, layer) * factor)
-    halt[:, rows] = score
-    weight = frows[0:1, rows] * (score - frows[target_row : target_row + 1, rows]) / sentences
-    term = exact(weight, layer)[0:1] * factor
+    score = jax.nn.sigmoid(jnp.sum(layer * vector, axis=-1, keepdims=True) * factor)
+    score_at[rows, :] = jnp.broadcast_to(score, (rows.size, score_at.shape[1]))
+    target = cols[rows, 0:1] if last else cols[rows, 4:5]
+    weight = cols[rows, 3:4] * (score - target) * (factor / sentences)
+    term = jnp.sum(weight * layer, axis=0, keepdims=True)
     exit_grad[...] = term if fresh else exit_grad[...] + term
 
 
@@ -479,95 +465,186 @@
     return here, later
 
 
+def halves(up):
+    hidden = up.shape[1]
+    return [slice(i * hidden // 2, (i + 1) * hidden // 2) for i in range(2)]
+
+
 def dense_forward_kernel(
-    sentences, meta, bank, x, gain, frows, final, halt, exit_grad, out, up, down, semaphores
+    sentences, meta, bank, x_in, gain, cols, final, active_out, slope_out, scores, exit_grad,
+    x, out, active, slope, up, down, semaphores
 ):
+    section = 1
     length, width = x.shape
     moves = Moves(meta, length, semaphores)
-    here, later = dense_weights(moves, bank, 1, up, down, width)
-    for wait in here:
-        wait()
+    x_here = moves.pair(x_in, x, FLAG_T)
+    here, later = dense_weights(moves, bank, section, up, down, width)
+    x_here()
 
     def part(rows, fresh):
         state = x[rows, :].astype(f32)
-        a = norm(state, gain[0:1, :]).astype(bf16)
-        active = gelu(dot(a, up[...])).astype(bf16)
+        a = norm(state, gain[section, 0:1]).astype(bf16)
+        if fresh:
+            for wait in here:
+                wait()
+        hidden = [dot(a, up[:, lanes]) for lanes in halves(up)]
+        for lanes, z in zip(halves(up), hidden):
+            value, gradient = gelu_both(z)
+            active[rows, lanes] = value.astype(bf16)
+            slope[rows, lanes] = gradient.astype(bf16)
         if fresh:
             for wait in later:
                 wait()
-        layer = state + dot(active, down[...])
+        layer = state + dot(active[rows, :], down[...])
         out[rows, :] = layer.astype(bf16)
-        exit_part(layer, gain[1:2, :], frows, rows, 1, halt, exit_grad, fresh, sentences)
+        exit_part(layer, gain[section, 1:2], cols, rows, False, scores, exit_grad, fresh, sentences)
 
     over(meta, FLAG_T, length, part)
     moves.away(out, final, FLAG_T)
+    moves.away(active, active_out, FLAG_T)
+    moves.away(slope, slope_out, FLAG_T)
     moves.finish()
 
 
-def dense_backward_kernel(sentences, final, meta, bank, x, gain, go_rows, frows, dh, before, dx_out, dw_out, dgain, *rest):
-    if final:
-        states, halt, exit_grad, out, *rest = rest
-        out[...] = jnp.zeros(out.shape, bf16)
-    else:
-        dgain[1:2, :] = before[...]
-    dx, dw, up, down, grad_up, grad_down, semaphores = rest
+def dense_gradients(moves, dw, dw_out, grad_up, grad_down, width):
+    parts = grad_up.shape[1] // width
+    for j in range(parts):
+        dw[parts + j] = grad_down[j * width : (j + 1) * width, :].astype(bf16)
+        moves.away(dw.at[parts + j], dw_out.at[parts + j])
+        dw[j] = grad_up[:, j * width : (j + 1) * width].astype(bf16)
+        moves.away(dw.at[j], dw_out.at[j])
+
+
+def accumulate(target, fresh, lanes, value):
+    target[lanes] = value if fresh else target[lanes] + value
+
+
+def dense_last_kernel(
+    sentences, meta, bank, x_in, gain, cols, dh_in, before, dx_out, dw_out, dgain, states, halt,
+    x, dh, scores, exit_grad, out, dx, dw, active, dhidden, up, down, grad_up, grad_down, semaphores
+):
+    section = 3
     length, width = x.shape
     moves = Moves(meta, length, semaphores)
-    here, later = dense_weights(moves, bank, 3 if final else 1, up, down, width)
-    parts = up.shape[1] // width
-    for wait in here:
-        wait()
+    x_here, dh_here = moves.pair(x_in, x, FLAG_T), moves.pair(dh_in, dh, FLAG_T)
+    here, later = dense_weights(moves, bank, section, up, down, width)
+    out[...] = jnp.zeros(out.shape, bf16)
+    scores[...] = jnp.zeros(scores.shape, f32)
+    x_here()
+    dh_here()
 
     def part(rows, fresh):
-        grad_out = dh[rows, :].astype(f32)
-        if final:
-            grad_out = jnp.where(go_rows[rows, 2:3] > 0.0, grad_out, 0.0)
-        go = go_rows[rows, int(final) : int(final) + 1]
+        go, own = cols[rows, 1:2], cols[rows, 2:3] > 0.0
+        grad_out = jnp.where(own, dh[rows, :].astype(f32), 0.0)
         state = x[rows, :].astype(f32)
-        a = norm(state, gain[0:1, :]).astype(bf16)
+        a = norm(state, gain[section, 0:1]).astype(bf16)
         dy = (go * grad_out).astype(bf16)
-        active, slope = gelu_both(dot(a, up[...]))
-        active = active.astype(bf16)
         if fresh:
-            for wait in later:
+            for wait in here + later:
                 wait()
-        dhidden = (slope * dot_nt(dy, down[...])).astype(bf16)
-        downs, ups = dot_tn(active, dy), dot_tn(a, dhidden)
-        if fresh:
-            grad_down[...] = downs
-            grad_up[...] = ups
-        else:
-            grad_down[...] += downs
-            grad_up[...] += ups
-        if final:
-            layer = state + go * dot(active, down[...])
-            out[rows, :] = jnp.where(go_rows[rows, 2:3] > 0.0, layer, 0.0).astype(bf16)
-            exit_part(layer, gain[1:2, :], frows, rows, 2, halt, exit_grad, fresh, sentences)
-        grad_x, grad_gain = norm_back(state, gain[0:1, :], dot_nt(dhidden, up[...]))
+        here_rows = slice(0, rows.size)
+        hidden = [dot(a, up[:, lanes]) for lanes in halves(up)]
+        for lanes, z in zip(halves(up), hidden):
+            grad = dot_nt(dy, down[lanes])
+            value, gradient = gelu_both(z)
+            active[here_rows, lanes] = value.astype(bf16)
+            dhidden[here_rows, lanes] = (gradient * grad).astype(bf16)
+        layer = state + go * dot(active[here_rows, :], down[...])
+        out[rows, :] = jnp.where(own, layer, 0.0).astype(bf16)
+        exit_part(layer, gain[section, 1:2], cols, rows, True, scores, exit_grad, fresh, sentences)
+        grad_x, grad_gain = norm_back(state, gain[section, 0:1], dot_nt(dhidden[here_rows, :], up[...]))
         dx[rows, :] = (grad_out + grad_x).astype(bf16)
         dgain[0:1, :] = grad_gain if fresh else dgain[0:1, :] + grad_gain
+        accumulate(grad_down, fresh, slice(None), dot_tn(active[here_rows, :], dy))
+        accumulate(grad_up, fresh, slice(None), dot_tn(a, dhidden[here_rows, :]))
 
     over(meta, FLAG_T, length, part)
     moves.away(dx, dx_out, FLAG_T)
-    if final:
-        moves.away(out, states)
-        dgain[1:2, :] = exit_grad[...]
-        mine = frows[3:4, :] > 0.0
-        halt[1:2, :] = jnp.where(mine, halt[1:2, :], 0.0)
-        halt[0:1, :] = jnp.where(mine, before[0:1, :], 0.0)
-    for j in range(parts):
-        dw[parts + j] = grad_down[j * width : (j + 1) * width, :].astype(bf16)
-        dw[j] = grad_up[:, j * width : (j + 1) * width].astype(bf16)
-        moves.away(dw.at[j], dw_out.at[j])
-        moves.away(dw.at[parts + j], dw_out.at[parts + j])
+    moves.away(out, states)
+    dgain[1:2, :] = exit_grad[...]
+    lane = lax.broadcasted_iota(i32, (BLOCK, 8), 1)
+    for i in range(length // BLOCK):
+        rows = slice(i * BLOCK, (i + 1) * BLOCK)
+        both = jnp.where(lane == 0, before[rows, :], scores[rows, :])
+        halt[:, rows] = jnp.where(cols[rows, 2:3] > 0.0, both, 0.0).T
+    dense_gradients(moves, dw, dw_out, grad_up, grad_down, width)
     moves.finish()
 
 
-def plan_kernel(sentences, row, core, seg, pad, mseg, mmask, depths, meta, info, frows, cols):
+def dense_backward_kernel(
+    meta, bank, x_in, gain, cols, dh_in, active_in, slope_in, exit_grad, dx_out, dw_out, dgain,
+    x, dh, dx, dw, active, slope, dhidden, up, down, grad_up, grad_down, semaphores
+):
+    section = 1
+    length, width = x.shape
+    moves = Moves(meta, length, semaphores)
+    dh_here = moves.pair(dh_in, dh, FLAG_T)
+    later, here = dense_weights(moves, bank, section, up, down, width)
+    here.append(moves.pair(slope_in, slope, FLAG_T))
+    here += [moves.pair(active_in, active, FLAG_T), moves.pair(x_in, x, FLAG_T)]
+    dgain[1:2, :] = exit_grad[...]
+    for wait in [dh_here] + here + later:
+        wait()
+
+    def part(rows, fresh):
+        dy = dh[rows, :]
+        grads = [dot_nt(dy, down[lanes]) for lanes in halves(up)]
+        for lanes, grad in zip(halves(up), grads):
+            dhidden[rows, lanes] = (slope[rows, lanes].astype(f32) * grad).astype(bf16)
+        state = x[rows, :].astype(f32)
+        a = norm(state, gain[section, 0:1]).astype(bf16)
+        grad_x, grad_gain = norm_back(state, gain[section, 0:1], dot_nt(dhidden[rows, :], up[...]))
+        dx[rows, :] = (dy.astype(f32) + grad_x).astype(bf16)
+        dgain[0:1, :] = grad_gain if fresh else dgain[0:1, :] + grad_gain
+        accumulate(grad_down, fresh, slice(None), dot_tn(active[rows, :], dy))
+        accumulate(grad_up, fresh, slice(None), dot_tn(a, dhidden[rows, :]))
+
+    over(meta, FLAG_T, length, part)
+    moves.away(dx, dx_out, FLAG_T)
+    dense_gradients(moves, dw, dw_out, grad_up, grad_down, width)
+    moves.finish()
+
+
+def widen_kernel(bank, dx, dmem, halt, bank_out, dx_out, dmem_out, halt_out):
+    bank_out[...] = bank[...].astype(f32)
+    dx_out[...] = dx[...].astype(f32)
+    dmem_out[...] = dmem[...].astype(f32)
+    halt_out[...] = halt[:, : halt_out.shape[1], :]
+
+
+def widen(bank, dx, dmem, halt):
+    steps = 8
+    span, width = bank.shape
+    micro, length, shares = dx.shape
+
+    def some(shape, *place):
+        return pl.BlockSpec(shape, lambda i: tuple(i if p else 0 for p in place))
+
+    rows = some((micro, length // steps, shares), 0, 1, 0)
+    whole = some((span // steps, width), 1, 0)
+    halting = (micro, 2, halt.shape[2])
+    return pl.pallas_call(
+        widen_kernel,
+        grid=(steps,),
+        out_shape=[jax.ShapeDtypeStruct(t.shape, f32) for t in (bank, dx, dmem)]
+        + [jax.ShapeDtypeStruct(halting, f32)],
+        in_specs=[whole, rows, rows, some(halt.shape, 0, 0, 0)],
+        out_specs=[whole, rows, rows, some(halting, 0, 0, 0)],
+        compiler_params=pltpu.CompilerParams(vmem_limit_bytes=60 * 2**20),
+        name="widen",
+    )(bank, dx, dmem, halt)
+
+
+def plan_kernel(sentences, row, core, seg, pad, mseg, mmask, depths, meta, info, cols):
     row, core = row[0], core[0]
-    length, slots = seg.shape[1], mseg.shape[1]
+    length, slots = seg.shape[2], mseg.shape[2]
     blocks = length // BLOCK
-    seg, pad, mseg, mmask = (t[pl.ds(row, 1), :] for t in (seg, pad, mseg, mmask))
+    micro = seg.shape[1]
+
+    def pick(table):
+        return table[row // micro, pl.ds(row % micro, 1), :]
+
+    seg, pad, mseg, mmask, depths = (pick(t) for t in (seg, pad, mseg, mmask, depths))
     number = lax.broadcasted_iota(i32, (sentences, length), 0)
     place = lax.broadcasted_iota(i32, (1, length), 1)
 
@@ -577,7 +654,7 @@
     square = lax.broadcasted_iota(i32, (sentences, sentences), 0) == lax.broadcasted_iota(
         i32, (sentences, sentences), 1
     )
-    depth_row = jnp.broadcast_to(depths[pl.ds(row, 1), :], (sentences, sentences))
+    depth_row = jnp.broadcast_to(depths, (sentences, sentences))
     depth_table = jnp.sum(jnp.where(square, depth_row, 0).astype(f32), axis=1, keepdims=True).astype(i32)
     mine = seg == number
     starts = count(seg < number)
@@ -658,8 +735,7 @@
     ones = jnp.ones((1, length), f32)
     kept, own = keep.astype(f32), owned.astype(f32)
     counted = jnp.where(pad == 1, own, 0.0)
-    frows[...] = jnp.concatenate([counted, (depth == 1).astype(f32), ones, own, ones, ones, ones, ones], axis=0)
-    by_row = jnp.concatenate([ones, kept, own, own, own, own, own, own], axis=0)
+    by_row = jnp.concatenate([ones, kept, own, counted, (depth == 1).astype(f32), own, own, own], axis=0)
     for i in range(blocks):
         cols[i * BLOCK : (i + 1) * BLOCK, :] = by_row[:, i * BLOCK : (i + 1) * BLOCK].T
 
@@ -671,13 +747,13 @@
 
 def make_plan(row, core, ints):
     seg, pad, mseg, mmask, depths = ints
-    length, sentences = seg.shape[1], depths.shape[1]
-    outs = [((length // BLOCK, 128), i32), ((8, length), i32), ((8, length), f32), ((length, 8), f32)]
+    length, sentences = seg.shape[-1], depths.shape[-1]
+    outs = [((length // BLOCK, 128), i32), ((8, length), i32), ((length, 8), f32)]
     return pl.pallas_call(
         functools.partial(plan_kernel, sentences),
         out_shape=[jax.ShapeDtypeStruct(*out) for out in outs],
         in_specs=[SMEM, SMEM] + [VMEM] * 5,
-        out_specs=[VMEM] * 4,
+        out_specs=[VMEM] * 3,
         compiler_params=pltpu.CompilerParams(vmem_limit_bytes=60 * 2**20),
         name="make_plan",
     )(row.astype(i32)[None], core.astype(i32)[None], seg, pad, mseg, mmask, depths)
@@ -698,7 +774,7 @@
 
 
 def attention_forward(layer, plan, bank, x, mem, gain, name):
-    meta, info, _, cols = plan
+    meta, info, cols = plan
     length, width = x.shape
     pairs = width // BLOCK
 
@@ -721,7 +797,7 @@
 
 
 def attention_backward(layer, plan, bank, x, mem, gain, saved, dh, dmem, name):
-    meta, info, _, cols = plan
+    meta, info, cols = plan
     length, width = x.shape
     pairs = width // BLOCK
 
@@ -744,49 +820,61 @@
     )
 
 
+def dense_shapes(bank, x):
+    length, width = x.shape
+    hidden = bank.shape[1] // 2 * width
+    return ((length, width), bf16), ((length, hidden), bf16), ((width, hidden), bf16), ((hidden, width), bf16)
+
+
 def dense_forward(plan, bank, x, gain, sentences, name):
-    meta, _, frows, _ = plan
+    meta, _, cols = plan
+    wide, inner, up, down = dense_shapes(bank, x)
+    outs = [(ANY, *wide), (ANY, *inner), (ANY, *inner), (VMEM, cols.shape, f32), (VMEM, (1, x.shape[1]), f32)]
+    return run(
+        functools.partial(dense_forward_kernel, sentences), [SMEM, ANY, ANY, VMEM, VMEM], outs,
+        [wide, wide, inner, inner, up, down], 24,
+        name, 4 * 10**9, meta, bank, x, gain, cols,
+    )
+
+
+def dense_last(plan, bank, x, gain, dh, before, sentences, name):
+    meta, _, cols = plan
+    wide, inner, up, down = dense_shapes(bank, x)
     length, width = x.shape
-    wide = ((length, width), bf16)
-    hidden = bank.shape[1] // 2 * width
-    outs = [(ANY, *wide), (VMEM, (8, length), f32), (VMEM, (1, width), f32)]
+    matrices = (bank.shape[1:], bf16)
+    outs = [(ANY, *wide), (ANY, *matrices), (VMEM, (2, width), f32), (ANY, *wide), (VMEM, (8, length), f32)]
+    inner = ((length * 5 // 8, inner[0][1]), bf16)
+    scratch = [wide, wide, (cols.shape, f32), ((1, width), f32), wide, wide, matrices, inner, inner, up, down,
+               (up[0], f32), (down[0], f32)]
     return run(
-        functools.partial(dense_forward_kernel, sentences), [SMEM, ANY, VMEM, VMEM, VMEM], outs,
-        [wide, ((width, hidden), bf16), ((hidden, width), bf16)], 16,
-        name, 4 * 10**9, meta, bank, x, gain, frows,
+        functools.partial(dense_last_kernel, sentences), [SMEM, ANY, ANY, VMEM, VMEM, ANY, VMEM], outs, scratch, 32,
+        name, 8 * 10**9, meta, bank, x, gain, cols, dh, before,
     )
 
 
-def dense_backward(plan, bank, x, gain, dh, before, sentences, final, name):
-    meta, _, frows, cols = plan
-    length, width = x.shape
-    wide = ((length, width), bf16)
-    hidden = bank.shape[1] // 2 * width
-    outs = [(ANY, *wide), (ANY, bank.shape[1:], bf16), (VMEM, (2, width), f32)]
-    scratch = [wide, (bank.shape[1:], bf16), ((width, hidden), bf16), ((hidden, width), bf16),
-               ((width, hidden), f32), ((hidden, width), f32)]
-    if final:
-        outs += [(ANY, *wide), (VMEM, (8, length), f32)]
-        scratch = [((1, width), f32), wide] + scratch
+def dense_backward(plan, bank, x, gain, dh, active, slope, exit_grad, name):
+    meta, _, cols = plan
+    wide, inner, up, down = dense_shapes(bank, x)
+    matrices = (bank.shape[1:], bf16)
+    outs = [(ANY, *wide), (ANY, *matrices), (VMEM, (2, x.shape[1]), f32)]
+    scratch = [wide, wide, wide, matrices, inner, inner, inner, up, down, (up[0], f32), (down[0], f32)]
     return run(
-        functools.partial(dense_backward_kernel, sentences, final), [SMEM, ANY] + [VMEM] * 6, outs, scratch, 24,
-        name, 8 * 10**9, meta, bank, x, gain, cols, frows, dh, before,
+        dense_backward_kernel, [SMEM, ANY, ANY, VMEM, VMEM, ANY, ANY, ANY, VMEM], outs, scratch, 32,
+        name, 8 * 10**9, meta, bank, x, gain, cols, dh, active, slope, exit_grad,
     )
 
 
 def row_forward_backward(row, core, x, mem, cotangent, bank, gains, ints):
     plan = make_plan(row, core, ints)
-    sentences = ints[-1].shape[1]
-    *saved0, zero = attention_forward(0, plan, bank, x, mem, gains[0], "attend_zero")
-    one, halt, exit0 = dense_forward(plan, bank, zero, gains[1], sentences, "dense_one")
-    *saved2, two = attention_forward(1, plan, bank, one, mem, gains[2], "attend_two")
-    dtwo, dw3, dgain3, states, halt = dense_backward(
-        plan, bank, two, gains[3], cotangent, halt, sentences, True, "dense_three"
-    )
-    done, dmem, dw2, dgain2 = attention_backward(1, plan, bank, one, mem, gains[2], saved2, dtwo, (), "attend_two_back")
-    dzero, dw1, dgain1 = dense_backward(plan, bank, zero, gains[1], done, exit0, sentences, False, "dense_one_back")
+    sentences = ints[-1].shape[-1]
+    *saved0, zero = attention_forward(0, plan, bank, x, mem, gains, "attend_zero")
+    one, active, slope, scores, exit0 = dense_forward(plan, bank, zero, gains, sentences, "dense_one")
+    *saved2, two = attention_forward(1, plan, bank, one, mem, gains, "attend_two")
+    dtwo, dw3, dgain3, states, halt = dense_last(plan, bank, two, gains, cotangent, scores, sentences, "dense_three")
+    done, dmem, dw2, dgain2 = attention_backward(1, plan, bank, one, mem, gains, saved2, dtwo, (), "attend_two_back")
+    dzero, dw1, dgain1 = dense_backward(plan, bank, zero, gains, done, active, slope, exit0, "dense_one_back")
     dx, dmem, dw0, dgain0 = attention_backward(
-        0, plan, bank, x, mem, gains[0], saved0, dzero, (dmem,), "attend_zero_back"
+        0, plan, bank, x, mem, gains, saved0, dzero, (dmem,), "attend_zero_back"
     )
     return states, halt, dx, dmem, [dw0, dw1, dw2, dw3], [dgain0, dgain1, dgain2, dgain3]
 
@@ -983,9 +1071,11 @@
     )(states, memory, cotangent, bank, gains, *ints)
 
 
-GROUPS = 8
+SIZES = (96,) * 10 + (64,)
+GROUPS = len(SIZES)
+LAGS = (0, 1, 2, 2, 3, 4, 5, 6, 7, 8)
 AHEAD = 2
-RESULTS = 7
+RESULTS = 11
 
 
 def add_rows(target, rows, *others):
@@ -996,7 +1086,7 @@
 
 
 def reduce_kernel(
-    dw0, dw1, dw2, dw3, gains, states, dx, dmem, halt,
+    dw0, dw1, dw2, dw3, gains0, gains1, gains2, gains3, states, dx, dmem, halt,
     bank, gains_sum, states_out, dx_out, dmem_out, halt_out,
     own, other, first, second, left, right, total, full, mine, theirs, score, scores,
     gain_parts, send, recv, home,
@@ -1032,24 +1122,23 @@
 
     span = dw0.shape[0]
     half = span // 2
-    quarter = half // 2
-    piece = quarter // GROUPS
+    offsets = [sum(SIZES[:g]) for g in range(GROUPS)]
     grads = (dw0, dw1, dw2, dw3)
 
     def at(g, side):
-        return side * quarter + g * piece
+        return 2 * offsets[g] + side * SIZES[g]
 
     loads, swaps = {}, {}
 
     def exchange(g):
+        size = 2 * SIZES[g]
+        rows = pl.ds(at(g, 0), size)
+        there = pl.ds(pl.multiple_of((1 - core) * half + at(g, 0), 32), size)
+        here = pl.ds(pl.multiple_of(core * half + at(g, 0), 32), size)
         for t in range(4):
-            for side in range(2):
-                rows = pl.ds(at(g, side), piece)
-                there = pl.ds(pl.multiple_of((1 - core) * half + at(g, side), piece), piece)
-                here = pl.ds(pl.multiple_of(core * half + at(g, side), piece), piece)
-                swaps[g, t, side] = go(grads[t].at[there], other.at[t, rows], sibling)
-                loads[g, t, side] = fetch(grads[t].at[here], own.at[t, rows])
-                loads[g, t, side].start()
+            swaps[g, t] = go(grads[t].at[there], other.at[t, rows], sibling)
+            loads[g, t] = fetch(grads[t].at[here], own.at[t, rows])
+            loads[g, t].start()
 
     for g in range(AHEAD):
         exchange(g)
@@ -1068,7 +1157,8 @@
             pl.when(holder)(copy.start)
 
     gain_steps = [sibling, across[0], across[1], pair, jump]
-    gain_parts[0] = gains[...]
+    for t, part in enumerate((gains0, gains1, gains2, gains3)):
+        gain_parts[0, 2 * t : 2 * t + 2] = part[...]
     gain_copies = []
 
     def gain_step(k):
@@ -1078,7 +1168,8 @@
         if k < len(gain_steps):
             gain_copies.append(go(gain_parts.at[2 * k], gain_parts.at[2 * k + 1], gain_steps[k]))
         else:
-            gains_sum[...] = gain_parts[2 * k]
+            for j in range(2):
+                gains_sum[j : j + 1, :] = gain_parts[2 * k, pl.ds(2 * s + j, 1), :]
 
     step1, step2, rs, ag = {}, {}, {}, {}
 
@@ -1086,40 +1177,37 @@
         if g + AHEAD < GROUPS:
             exchange(g + AHEAD)
         for t in range(4):
-            for side in range(2):
-                swaps[g, t, side].wait_recv()
-                loads[g, t, side].wait()
-                rows = pl.ds(at(g, side), piece)
-                add_rows(own, (t, rows), (other, (t, rows)))
+            swaps[g, t].wait_recv()
+            loads[g, t].wait()
+            rows = pl.ds(at(g, 0), 2 * SIZES[g])
+            add_rows(own, (t, rows), (other, (t, rows)))
         for side in range(2):
-            rows = pl.ds(at(g, side), piece)
+            rows = pl.ds(at(g, side), SIZES[g])
             for n, rel in enumerate((3, 1 + side)):
-                step1[g, side, n] = go(own.at[chips[rel], rows], first.at[g, side, n], across[side])
+                step1[g, side, n] = go(own.at[chips[rel], rows], first.at[n, rows], across[side])
 
     def plane_second(g):
         for side in range(2):
-            rows = pl.ds(at(g, side), piece)
+            rows = pl.ds(at(g, side), SIZES[g])
             for n, rel in enumerate((2 - side, 0)):
                 step1[g, side, n].wait_recv()
-                add_rows(own, (chips[rel], rows), (first, (g, side, n)))
+                add_rows(own, (chips[rel], rows), (first, (n, rows)))
                 if n == 0:
-                    step2[g, side] = go(own.at[chips[rel], rows], second.at[g, side], across[1 - side])
+                    step2[g, side] = go(own.at[chips[rel], rows], second.at[rows], across[1 - side])
 
     def plane_third(g):
         for side in range(2):
             step2[g, side].wait_recv()
-            rows = pl.ds(at(g, side), piece)
-            value = own[s, rows].astype(f32) + second[g, side].astype(f32)
-            total[g, pl.ds(side * piece, piece)] = value.astype(bf16)
-
-    wide = 2 * piece
-    shard = wide // 4
-
-    def span_of(k0, k1):
-        return pl.ds(k0 * shard, (k1 - k0) * shard)
+            rows = pl.ds(at(g, side), SIZES[g])
+            value = own[s, rows].astype(f32) + second[rows].astype(f32)
+            total[pl.ds(2 * offsets[g] + side * SIZES[g], SIZES[g])] = value.astype(bf16)
+
+    def span_of(g, k0, k1):
+        shard = SIZES[g] // 2
+        return pl.ds(2 * offsets[g] + k0 * shard, (k1 - k0) * shard)
 
     def share(kind, g, low, high, src, dst, device):
-        return push(src.at[g, span_of(low, high)], dst.at[g, span_of(low, high)], device)
+        return push(src.at[span_of(g, low, high)], dst.at[span_of(g, low, high)], device)
 
     def line_sums(g):
         for z in range(3):
@@ -1127,18 +1215,18 @@
             rs[g, "down", z + 1] = share("down", g, 0, z + 1, total, left, down)
         for k in range(4):
             for z in range(k, 3):
-                ag[g, "up", z, k] = push(full.at[g, span_of(k, k + 1)], full.at[g, span_of(k, k + 1)], up)
+                ag[g, "up", z, k] = push(full.at[span_of(g, k, k + 1)], full.at[span_of(g, k, k + 1)], up)
             for z in range(1, k + 1):
-                ag[g, "down", z, k] = push(full.at[g, span_of(k, k + 1)], full.at[g, span_of(k, k + 1)], down)
+                ag[g, "down", z, k] = push(full.at[span_of(g, k, k + 1)], full.at[span_of(g, k, k + 1)], down)
 
     def at_layer(z, action):
         pl.when(layer == z)(action)
 
     def close(g, k, *others):
-        value = total[g, span_of(k, k + 1)].astype(f32)
+        value = total[span_of(g, k, k + 1)].astype(f32)
         for other_ in others:
-            value = value + other_[g, span_of(k, k + 1)].astype(f32)
-        full[g, span_of(k, k + 1)] = value.astype(bf16)
+            value = value + other_[span_of(g, k, k + 1)].astype(f32)
+        full[span_of(g, k, k + 1)] = value.astype(bf16)
 
     def line_1(g):
         line_sums(g)
@@ -1148,12 +1236,12 @@
     def line_2(g):
         def second_layer():
             rs[g, "up", 0].wait_recv()
-            add_rows(total, (g, span_of(2, 4)), (right, (g, span_of(2, 4))))
+            add_rows(total, span_of(g, 2, 4), (right, span_of(g, 2, 4)))
             rs[g, "up", 1].start()
 
         def third_layer():
             rs[g, "down", 3].wait_recv()
-            add_rows(total, (g, span_of(0, 2)), (left, (g, span_of(0, 2))))
+            add_rows(total, span_of(g, 0, 2), (left, span_of(g, 0, 2)))
             rs[g, "down", 2].start()
 
         at_layer(1, second_layer)
@@ -1162,7 +1250,7 @@
     def line_3(g):
         def third_layer():
             rs[g, "up", 1].wait_recv()
-            add_rows(total, (g, span_of(3, 4)), (right, (g, span_of(3, 4))))
+            add_rows(total, span_of(g, 3, 4), (right, span_of(g, 3, 4)))
             rs[g, "up", 2].start()
             close(g, 2, right, left)
             ag[g, "up", 2, 2].start()
@@ -1170,7 +1258,7 @@
 
         def second_layer():
             rs[g, "down", 2].wait_recv()
-            add_rows(total, (g, span_of(0, 1)), (left, (g, span_of(0, 1))))
+            add_rows(total, span_of(g, 0, 1), (left, span_of(g, 0, 1)))
             rs[g, "down", 1].start()
             close(g, 1, right, left)
             ag[g, "up", 1, 1].start()
@@ -1248,13 +1336,12 @@
     def line_7(g):
         at_layer(0, lambda: ag[g, "down", 1, 3].wait_recv())
         at_layer(3, lambda: ag[g, "up", 2, 0].wait_recv())
-        for side in range(2):
-            here = pl.ds(pl.multiple_of(core * half + at(g, side), piece), piece)
-            rows = full.at[g, pl.ds(side * piece, piece)]
-            finals[g, side] = go(rows, bank.at[here], sibling)
-            copy = fetch(rows, bank.at[here])
-            copy.start()
-            ends.append(copy)
+        here = pl.ds(pl.multiple_of(core * half + at(g, 0), 32), 2 * SIZES[g])
+        rows = full.at[pl.ds(2 * offsets[g], 2 * SIZES[g])]
+        finals[g] = go(rows, bank.at[here], sibling)
+        copy = fetch(rows, bank.at[here])
+        copy.start()
+        ends.append(copy)
 
     handed = []
 
@@ -1291,9 +1378,8 @@
                 handed.append((rel, copy))
 
     stages = [plane_first, plane_second, plane_third, line_1, line_2, line_3, line_4, line_5, line_6, line_7]
-    lags = [0, 1, 2, 2, 3, 3, 4, 4, 5, 5]
-    for tick in range(GROUPS + 6):
-        for stage, lag in zip(stages, lags):
+    for tick in range(GROUPS + LAGS[-1]):
+        for stage, lag in zip(stages, LAGS):
             if 0 <= tick - lag < GROUPS:
                 stage(tick - lag)
         if tick <= len(gain_steps):
@@ -1327,33 +1413,32 @@
     length, width = states.shape
     span = dw[0].shape[0]
     half = span // 2
-    piece = half // 2 // GROUPS
     shares = width // sections
     micro = 2
     share = jax.ShapeDtypeStruct((micro, length, shares), bf16)
-    outs = [jax.ShapeDtypeStruct((span, width), bf16), jax.ShapeDtypeStruct(gains.shape, f32), share, share, share,
+    outs = [jax.ShapeDtypeStruct((span, width), bf16), jax.ShapeDtypeStruct((2, width), f32), share, share, share,
             jax.ShapeDtypeStruct((micro, halt.shape[0], length // sections), f32)]
     copies = 8 * GROUPS + 4 + 5 + (4 + 2 + 6 + 12 + 2) * GROUPS + 12
     scratch = [
         pltpu.VMEM((4, half, width), bf16), pltpu.VMEM((4, half, width), bf16),
-        pltpu.VMEM((GROUPS, 2, 2, piece, width), bf16), pltpu.VMEM((GROUPS, 2, piece, width), bf16),
-        pltpu.VMEM((GROUPS, 2 * piece, width), bf16), pltpu.VMEM((GROUPS, 2 * piece, width), bf16),
-        pltpu.VMEM((GROUPS, 2 * piece, width), bf16), pltpu.VMEM((GROUPS, 2 * piece, width), bf16),
+        pltpu.VMEM((2, half, width), bf16), pltpu.VMEM((half, width), bf16),
+        pltpu.VMEM((half, width), bf16), pltpu.VMEM((half, width), bf16),
+        pltpu.VMEM((half, width), bf16), pltpu.VMEM((half, width), bf16),
         pltpu.VMEM((3, length, width), bf16), pltpu.VMEM((3, length, width), bf16),
         pltpu.VMEM(halt.shape, f32), pltpu.VMEM(halt.shape, f32),
-        pltpu.VMEM((11,) + gains.shape, f32),
+        pltpu.VMEM((11, 2 * sections, width), f32),
         pltpu.SemaphoreType.DMA((copies,)), pltpu.SemaphoreType.DMA((copies,)),
         pltpu.SemaphoreType.DMA((8 * GROUPS + 4 + 2 * GROUPS + 4,)),
     ]
     return pl.pallas_call(
         reduce_kernel,
         out_shape=outs,
-        in_specs=[ANY] * 4 + [VMEM] + [ANY] * 4,
+        in_specs=[ANY] * 4 + [VMEM] * 4 + [ANY] * 4,
         out_specs=[ANY, VMEM, ANY, ANY, ANY, ANY],
         scratch_shapes=scratch,
-        compiler_params=pltpu.CompilerParams(collective_id=1, has_side_effects=True, vmem_limit_bytes=52 * 2**20),
+        compiler_params=pltpu.CompilerParams(collective_id=1, has_side_effects=True, vmem_limit_bytes=60 * 2**20),
         name="reduce_all",
-    )(*dw, gains, states, dx, dmem, halt)
+    )(*dw, *gains, states, dx, dmem, halt)
 
 
 def swap_cores(value):
@@ -1406,32 +1491,25 @@
             states_in, memory, cotangent, weight_bank[0].reshape(-1, width), gain_bank[0], ints
         )
         bank = bank.reshape((sections,) + matrices)
-        ints, row = [t.reshape(-1, t.shape[-1]) for t in ints], section
+        row = section
     else:
         (x, mem, top), bank, gains, ints = gather_plain(
             states_in, memory, cotangent, weight_bank[0], gain_bank[0], ints
         )
-        ints, row = [t[None] for t in ints], jnp.zeros((), i32)
+        ints, row = [t[None, None] for t in ints], jnp.zeros((), i32)
     states, halt, dx, dmem, dw, dgains = row_forward_backward(
-        row, core, x, mem, top, bank, [gains[i] for i in range(sections)], ints
+        row, core, x, mem, top, bank, gains, ints
     )
     if near:
         grads = [t.reshape(-1, width) for t in dw]
         bank, gain_sum, states, dx, dmem, halt = reduce_all(
-            grads, jnp.concatenate(dgains), states, dx, dmem, halt, sections
+            grads, dgains, states, dx, dmem, halt, sections
         )
-        bank = bank.reshape(matrices)
-        gain_sum = lax.dynamic_index_in_dim(gain_sum.reshape(sections, 2, width), section, 0, keepdims=False)
     else:
         bank, gain_sum, states, dx, dmem, halt = reduce_plain(dw, dgains, states, dx, dmem, halt)
-    return (
-        states,
-        halt[:, :2],
-        dx.astype(f32),
-        dmem.astype(f32),
-        bank.astype(f32)[None],
-        gain_sum[None],
-    )
+        bank = bank.reshape(-1, width)
+    bank, dx, dmem, halt = widen(bank, dx, dmem, halt)
+    return states, halt, dx, dmem, bank.reshape((1,) + matrices), gain_sum[None]
 
 
 def solution(mesh):

time: 392 us -> 362 us (0.923)
  the two profiles are of different devices: /device:TPU:5 before, /device:TPU:0 now
where the time goes in v2:
time: 362 us; the launch traced here: 356 us
  Pallas kernels  353 us (98%)
    pallas_call x7, Pallas kernels, run(): pl.pallas_call(kernel, out_shape=[jax.ShapeDtypeStruct(shape, dtype) for...  134 us
    pallas_call x1, Pallas kernels, reduce_all(): pl.pallas_call(reduce_kernel, out_shape=outs, in_specs=[ANY] * 4 + [VMEM]...  132 us
    pallas_call x1, Pallas kernels, gather_all(): pl.pallas_call(gather_kernel, out_shape=outs, in_specs=[ANY] * 10, out_sp...  76.3 us
    pallas_call x1, Pallas kernels, widen(): pl.pallas_call(widen_kernel, grid=(steps,), out_shape=[jax.ShapeDtypeStru...  7.85 us

profile of v2, /device:TPU:0, one launch (start us, length us, event | category | flops | bytes accessed | tf_op | source)
XLA Modules:
  0.0 355.9 jit_solution(8581782052840126121)
XLA Ops:
  0.6 76.3 %gather_all.1 = (bf16[1024,512]{1,0:T(8,128)(2,1)}, bf16[1024,512]{1,0:T(8,128)(2,1)}, bf16[1024,512]{1,0:T(8,128)(2,1)}, bf16[16384,512]{1,0:T(8,128)(2,1)}, f3...) custom-call(bf16[2,1024,128]{2,1,0:T(8,128)(2,1)} %states.1, ...), custom_call_target="tpu_custom_call" | custom-call | tf_op jit(solution)/shard_map/gather_all/pallas_call | solution.py:1062
  76.9 2.5 make_plan.1
  79.5 17.5 %attend_zero.1 = (bf16[1024,1536]{1,0:T(8,128)(2,1)}, bf16[1024,512]{1,0:T(8,128)(2,1)}, f32[8,1024]{1,0:T(8,128)}, f32[1024,512]{1,0:T(8,128)}, bf16[1024,512]{...) custom-call(s32[8,128]{1,0:T(8,128)} %get-tuple-element.73.meta, ...), custom_call_target="tpu_custom_call" | custom-call | flops 6000000000 | bytes 20971520 | tf_op jit(solution)/shard_map/attend_zero/pallas_call | solution.py:763
  97.0 12.0 %dense_one.1 = (bf16[1024,512]{1,0:T(8,128)(2,1)}, bf16[1024,2048]{1,0:T(8,128)(2,1)}, bf16[1024,2048]{1,0:T(8,128)(2,1)}, f32[1024,8]{1,0:T(8,128)}, f32[1,512]{1,0:T(1,128)}) custom-call(s32[8,128]{1,0:T(8,128)} %get-tuple-element.73.meta, bf16[4,8,512,512]{3,2,1,0:T(8,128)(2,1)} %bitcast.12, bf16[1024,512]{1,0:T(8,128)(2,1)} %get-tuple-element.88.x_in, ...), custom_call_target="tpu_custom_call" | custom-call | flops 4000000000 | bytes 20971520 | tf_op jit(solution)/shard_map/dense_one/pallas_call | solution.py:763
  109.0 17.1 %attend_two.1 = (bf16[1024,1536]{1,0:T(8,128)(2,1)}, bf16[1024,512]{1,0:T(8,128)(2,1)}, f32[8,1024]{1,0:T(8,128)}, f32[1024,512]{1,0:T(8,128)}, bf16[1024,512]{1...) custom-call(s32[8,128]{1,0:T(8,128)} %get-tuple-element.73.meta, ...), custom_call_target="tpu_custom_call" | custom-call | flops 6000000000 | bytes 20971520 | tf_op jit(solution)/shard_map/attend_two/pallas_call | solution.py:763
  126.1 18.1 %dense_three.1 = (bf16[1024,512]{1,0:T(8,128)(2,1)}, bf16[8,512,512]{2,1,0:T(8,128)(2,1)}, f32[2,512]{1,0:T(2,128)}, bf16[1024,512]{1,0:T(8,128)(2,1)}, f32[8,1024]{1,0:T(8,128)}) custom-call(s32[8,128]{1,0:T(8,128)} %get-tuple-element.73.meta, bf16[4,8,512,512]{3,2,1,0:T(8,128)(2,1)} %bitcast.14, bf16[1024,512]{1,0:T(8,128)(2,1)} %get-tuple-element.98.x_in, ...), custom_call_target="tpu_custom_call" | custom-call | flops 8000000000 | bytes 20971520 | tf_op jit(solution)/shard_map/dense_three/pallas_call | solution.py:763
  144.3 27.5 %attend_two_back.1 = (bf16[1024,512]{1,0:T(8,128)(2,1)}, bf16[1024,512]{1,0:T(8,128)(2,1)}, bf16[8,512,512]{2,1,0:T(8,128)(2,1)}, f32[2,512]{1,0:T(2,128)}) custom-call(s32[8,128]{1,0:T(8,128)} %get-tuple-element.73.meta, bf16[4,8,512,512]{3,2,1,0:T(8,128)(2,1)} %bitcast.15, bf16[1024,512]{1,0:T(8,128)(2,1)} %get-tuple-element.89.x_in, ...), custom_call_target="tpu_custom_call" | custom-call | flops 12000000000 | bytes 20971520 | tf_op jit(solution)/shard_map/attend_two_back/pallas_call | solution.py:763
  171.7 14.5 %dense_one_back.1 = (bf16[1024,512]{1,0:T(8,128)(2,1)}, bf16[8,512,512]{2,1,0:T(8,128)(2,1)}, f32[2,512]{1,0:T(2,128)}) custom-call(s32[8,128]{1,0:T(8,128)} %get-tuple-element.73.meta, bf16[4,8,512,512]{3,2,1,0:T(8,128)(2,1)} %bitcast.16, bf16[1024,512]{1,0:T(8,128)(2,1)} %get-tuple-element.88.x_in, f32[4,2,512]{2,1,0:T(2,128)} %get-tuple-element.77.gain, ...), custom_call_target="tpu_custom_call" | custom-call | flops 8000000000 | bytes 20971520 | tf_op jit(solution)/shard_map/dense_one_back/pallas_call | solution.py:763
  186.2 27.8 %attend_zero_back.1 = (bf16[1024,512]{1,0:T(8,128)(2,1)}, bf16[1024,512]{1,0:T(8,128)(2,1)}, bf16[8,512,512]{2,1,0:T(8,128)(2,1)}, f32[2,512]{1,0:T(2,128)}) custom-call(s32[8,128]{1,0:T(8,128)} %get-tuple-element.73.meta, bf16[4,8,512,512]{3,2,1,0:T(8,128)(2,1)} %bitcast.17, bf16[1024,512]{1,0:T(8,128)(2,1)} %get-tuple-element.75.x_in, ...), custom_call_target="tpu_custom_call" | custom-call | flops 12000000000 | bytes 20971520 | tf_op jit(solution)/shard_map/attend_zero_back/pallas_call | solution.py:763
  214.0 132.1 %reduce_all.1 = (bf16[4096,512]{1,0:T(8,128)(2,1)}, f32[2,512]{1,0:T(2,128)}, bf16[2,1024,128]{2,1,0:T(8,128)(2,1)}, bf16[2,1024,128]{2,1,0:T(8,128)(2,1)}, bf16...) custom-call(bf16[4096,512]{1,0:T(8,128)(2,1)} %bitcast.22, bf16[4096,512]{1,0:T(8,128)(2,1)} %bitcast.21, ...), custom_call_target="tpu_custom_call" | custom-call | tf_op jit(solution)/shard_map/reduce_all/pallas_call | solution.py:1433
  346.2 0.0 copy-start
  346.2 0.0 copy-start.1
  346.2 7.8 %widen.1 = (f32[4096,512]{1,0:T(8,128)}, f32[2,1024,128]{2,1,0:T(8,128)}, f32[2,1024,128]{2,1,0:T(8,128)}, f32[2,2,256]{2,1,0:T(2,128)}) custom-call(bf16[4096,512]{1,0:T(8,128)(2,1)} %get-tuple-element.121.bank, bf16[2,1024,128]{2,1,0:T(8,128)(2,1)} %get-tuple-element.122.dx, bf16[2,1024,128]{2,1,0:T(8,128)(2,1)} %get-tuple-element.123.dmem, ...), custom_call_target="tpu_custom_call" | custom-call | tf_op jit(solution)/shard_map/widen/pallas_call | solution.py:626
  354.0 0.0 copy-done
  354.0 0.8 copy.18
  354.8 0.0 copy-done.1
  354.8 0.6 copy.19
Async XLA Ops:
  346.2 7.9 %copy-start = (bf16[2,1024,128]{2,1,0:T(8,128)(2,1)S(1)}, bf16[2,1024,128]{2,1,0:T(8,128)(2,1)}, u32[]{:S(2)}) copy-start(bf16[2,1024,128]{2,1,0:T(8,128)(2,1)} %get-tuple-element.136) | copy-start | bytes 1572868
  346.2 8.7 %copy-start.1 = (f32[2,512]{1,0:T(2,128)S(1)}, f32[2,512]{1,0:T(2,128)}, u32[]{:S(2)}) copy-start(f32[2,512]{1,0:T(2,128)} %get-tuple-element.129) | copy-start | bytes 12292

commit v3 on v2

--- a/solution.py
+++ b/solution.py
@@ -93,22 +93,39 @@
         return copy.wait
 
     def pair(self, src, dst, flag):
+        start, wait = self.parts(src, dst, flag)
+        start(True)
+        pl.when(self.meta[0, flag] == 1)(lambda: start(False))
+        return wait
+
+    def parts(self, src, dst, flag):
         first, second = (self.copy(src.at[rows], dst.at[rows]) for rows in self.rows)
-        first.start()
-        pl.when(self.meta[0, flag] == 1)(second.start)
+
+        def start(fresh):
+            (first if fresh else second).start()
 
         def wait():
             first.wait()
             pl.when(self.meta[0, flag] == 1)(second.wait)
 
-        return wait
+        return start, wait
 
     def away(self, src, dst, flag=None):
         self.leaving.append(self.whole(src, dst) if flag is None else self.pair(src, dst, flag))
 
+    def away_by_part(self, src, dst, flag):
+        start, wait = self.parts(src, dst, flag)
+        self.leaving.append(wait)
+        return start
+
     def finish(self):
-        for wait in self.leaving:
-            wait()
+        all_of(*self.leaving)
+        self.leaving = []
+
+
+def all_of(*waits):
+    for wait in waits:
+        wait()
 
 
 def block(i):
@@ -217,20 +234,27 @@
 
             def one_window(n, _):
                 keys, bias = key_window(meta, kind, top, i, n, low, high)
-                these = [k[keys, lanes_of(k_at, p)] for p in range(pairs)]
-                scores = [dot_nt(these[p], both_q[p]) for p in range(pairs)]
-                grad_probs = [dot_nt(v[keys, lanes_of(v_at, p)], both_o[p]) for p in range(pairs)]
-                probs = [jnp.exp(scores[p] + bias - two_rows(lse, p, rows)) for p in range(pairs)]
-                grad_scores = [
-                    (probs[p] * (grad_probs[p] - two_rows(delta, p, rows))).astype(bf16) for p in range(pairs)
-                ]
-                grads_v = [dot(probs[p].astype(bf16), both_o[p]) for p in range(pairs)]
-                grads_k = [dot(grad_scores[p], both_q[p]) for p in range(pairs)]
-                grads_q = [dot_tn(these[p], grad_scores[p]) for p in range(pairs)]
+                def products(p):
+                    return dot_nt(k[keys, lanes_of(k_at, p)], both_q[p]), dot_nt(v[keys, lanes_of(v_at, p)], both_o[p])
+
+                def soften(p, score, grad):
+                    prob = jnp.exp(score + bias - two_rows(lse, p, rows))
+                    return prob.astype(bf16), (prob * (grad - two_rows(delta, p, rows))).astype(bf16)
+
+                def mix(p, prob, grad_score):
+                    dv[keys, lanes_of(0, p)] += dot(prob, both_o[p])
+                    dk[keys, lanes_of(0, p)] += dot(grad_score, both_q[p])
+                    sums[p] += both_blocks(dot_tn(k[keys, lanes_of(k_at, p)], grad_score))
+
+                tiles = {0: products(0), 1: products(1)}
+                soft = {}
                 for p in range(pairs):
-                    dv[keys, lanes_of(0, p)] += grads_v[p]
-                    dk[keys, lanes_of(0, p)] += grads_k[p]
-                    sums[p] += both_blocks(grads_q[p])
+                    soft[p] = soften(p, *tiles[p])
+                    if p + 2 < pairs:
+                        tiles[p + 2] = products(p + 2)
+                    if p > 0:
+                        mix(p - 1, *soft[p - 1])
+                mix(pairs - 1, *soft[pairs - 1])
                 return 0
 
             lax.fori_loop(0, count, one_window, 0)
@@ -242,209 +266,376 @@
     lax.fori_loop(meta[0, FIRST], meta[0, LAST], one_block, 0)
 
 
-def attention_forward_kernel(
-    layer, meta, bank, x_in, mem_in, gain, go_rows, info,
-    qkv_out, o1_out, l1, mid_out, q2_out, kv_out, o2_out, l2, final,
-    x, mem, qkv, o1, mid, q2, kv, o2, out, wide, third, fourth, pairw, last, both_q, peaks, totals, sums, semaphores,
+def side_by_side(moves, bank, section, first, place):
+    width = place.shape[0]
+    return [
+        moves.whole(bank.at[section, first + j], place.at[:, j * width : (j + 1) * width])
+        for j in range(place.shape[1] // width)
+    ]
+
+
+def stacked(moves, bank, section, first, place):
+    width = place.shape[1]
+    return [
+        moves.whole(bank.at[section, first + j], place.at[j * width : (j + 1) * width])
+        for j in range(place.shape[0] // width)
+    ]
+
+
+def forward_kernel(
+    sentences, meta, bank, x_in, mem_in, gain, cols, info,
+    qkv_out0, o1_out0, l1_0, mid_out0, q2_out0, kv_out0, o2_out0, l2_0, zero_out,
+    one_out, active_out, slope_out, scores, exit_grad,
+    qkv_out2, o1_out2, l1_2, mid_out2, q2_out2, kv_out2, o2_out2, l2_2, two_out,
+    x, mem, qkv, o1, mid, q2, kv, o2, zero, one, two, active, slope,
+    wide, third, fourth, pairw, last, up, down, both_q, peaks, totals, sums, semaphores,
 ):
     length, width = x.shape
-    kind, flag_m, top_m = 4 * layer, FLAG_M + 2 * layer, TOP_M + 2 * layer
     moves = Moves(meta, length, semaphores)
-    section = 2 * layer
-    x_here = moves.pair(x_in, x, FLAG_T)
-    self_here = [moves.whole(bank.at[section, j], wide.at[:, j * width : (j + 1) * width]) for j in range(3)]
-    mem_here = moves.pair(mem_in, mem, flag_m)
-    pair_here = [moves.whole(bank.at[section, 5 + j], pairw.at[:, j * width : (j + 1) * width]) for j in range(2)]
-    rest_here = [moves.whole(bank.at[section, j], place) for j, place in ((3, third), (4, fourth), (7, last))]
-    go = (lambda rows: go_rows[rows, layer : layer + 1])
-    x_here()
-    for wait in self_here:
-        wait()
-
-    def self_in(rows, _):
-        a = norm(x[rows, :].astype(f32), gain[section, 0:1]).astype(bf16)
-        both = dot(a, wide[...])
-        qkv[rows, :width] = (both[:, :width] * 0.125).astype(bf16)
-        qkv[rows, width:] = both[:, width:].astype(bf16)
-        o1[rows, :] = jnp.zeros((rows.size, width), bf16)
-        o2[rows, :] = jnp.zeros((rows.size, width), bf16)
-
-    over(meta, FLAG_T, length, self_in)
-    moves.away(qkv, qkv_out, FLAG_T)
-    mem_here()
-    for wait in pair_here:
-        wait()
-
-    def memory_in(rows, _):
-        kv[rows, :] = dot(mem[rows, :], pairw[...]).astype(bf16)
-
-    over(meta, flag_m, length, memory_in)
-    moves.away(kv, kv_out, flag_m)
-    l1[...] = jnp.zeros(l1.shape, f32)
-    l2[...] = jnp.zeros(l2.shape, f32)
-    attend(
-        meta, SELF + kind, TOP_T, info, 0, (qkv, 0), (qkv, width), (qkv, 2 * width), o1, l1,
-        both_q, peaks, totals, sums,
+    here = {"x": [moves.pair(x_in, x, FLAG_T)], "self": side_by_side(moves, bank, 0, 0, wide)}
+
+    def ready(*names):
+        for name in names:
+            all_of(*here.pop(name))
+
+    def attention(layer, state_in, out, saved, final):
+        qkv_out, o1_out, l1, mid_out, q2_out, kv_out, o2_out, l2 = saved
+        kind, flag_m, top_m = 4 * layer, FLAG_M + 2 * layer, TOP_M + 2 * layer
+        section = 2 * layer
+
+        def go(rows):
+            return cols[rows, layer : layer + 1]
+
+        ready("self")
+
+        def self_in(rows, _):
+            a = norm(state_in[rows, :].astype(f32), gain[section, 0:1]).astype(bf16)
+            both = dot(a, wide[...])
+            qkv[rows, :width] = (both[:, :width] * 0.125).astype(bf16)
+            qkv[rows, width:] = both[:, width:].astype(bf16)
+            o1[rows, :] = jnp.zeros((rows.size, width), bf16)
+            o2[rows, :] = jnp.zeros((rows.size, width), bf16)
+
+        over(meta, FLAG_T, length, self_in)
+        moves.away(qkv, qkv_out, FLAG_T)
+        if layer == 0:
+            here["self"] = side_by_side(moves, bank, 2, 0, wide)
+        ready("pair")
+
+        def memory_in(rows, _):
+            kv[rows, :] = dot(mem[rows, :], pairw[...]).astype(bf16)
+
+        over(meta, flag_m, length, memory_in)
+        moves.away(kv, kv_out, flag_m)
+        if layer == 0:
+            here["pair"] = side_by_side(moves, bank, 2, 5, pairw)
+            here["up"] = side_by_side(moves, bank, 1, 0, up)
+            here["down"] = stacked(moves, bank, 1, 4, down)
+        l1[...] = jnp.zeros(l1.shape, f32)
+        l2[...] = jnp.zeros(l2.shape, f32)
+        attend(
+            meta, SELF + kind, TOP_T, info, 0, (qkv, 0), (qkv, width), (qkv, 2 * width), o1, l1,
+            both_q, peaks, totals, sums,
+        )
+        moves.away(o1, o1_out, FLAG_T)
+        ready("middle")
+
+        def cross_in(rows, _):
+            state = state_in[rows, :].astype(f32) + go(rows) * dot(o1[rows, :], third[...])
+            mid[rows, :] = state
+            a = norm(state, gain[section, 1:2]).astype(bf16)
+            q2[rows, :] = (dot(a, fourth[...]) * 0.125).astype(bf16)
+
+        over(meta, FLAG_T, length, cross_in)
+        moves.away(mid, mid_out, FLAG_T)
+        moves.away(q2, q2_out, FLAG_T)
+        if layer == 0:
+            here["middle"] = [moves.whole(bank.at[2, j], place) for j, place in ((3, third), (4, fourth))]
+        attend(
+            meta, CROSS + kind, top_m, info, 2, (q2, 0), (kv, 0), (kv, width), o2, l2, both_q, peaks, totals, sums
+        )
+        moves.away(o2, o2_out, FLAG_T)
+        ready("last")
+
+        def finish(rows, _):
+            out[rows, :] = (mid[rows, :] + go(rows) * dot(o2[rows, :], last[...])).astype(bf16)
+
+        over(meta, FLAG_T, length, finish)
+        moves.away(out, final, FLAG_T)
+        if layer == 0:
+            here["last"] = [moves.whole(bank.at[2, 7], last)]
+
+    ready("x")
+    here["memory"] = [moves.pair(mem_in, mem, FLAG_M)]
+    here["pair"] = side_by_side(moves, bank, 0, 5, pairw)
+    here["middle"] = [moves.whole(bank.at[0, j], place) for j, place in ((3, third), (4, fourth))]
+    here["last"] = [moves.whole(bank.at[0, 7], last)]
+    here["pair"] += here.pop("memory")
+    attention(
+        0, x, zero, (qkv_out0, o1_out0, l1_0, mid_out0, q2_out0, kv_out0, o2_out0, l2_0), zero_out
     )
-    moves.away(o1, o1_out, FLAG_T)
-    for wait in rest_here:
-        wait()
-
-    def cross_in(rows, _):
-        state = x[rows, :].astype(f32) + go(rows) * dot(o1[rows, :], third[...])
-        mid[rows, :] = state
-        a = norm(state, gain[section, 1:2]).astype(bf16)
-        q2[rows, :] = (dot(a, fourth[...]) * 0.125).astype(bf16)
-
-    over(meta, FLAG_T, length, cross_in)
-    moves.away(mid, mid_out, FLAG_T)
-    moves.away(q2, q2_out, FLAG_T)
-    attend(
-        meta, CROSS + kind, top_m, info, 2, (q2, 0), (kv, 0), (kv, width), o2, l2, both_q, peaks, totals, sums
+    kept = [moves.parts(src, dst, FLAG_T) for src, dst in ((active, active_out), (slope, slope_out))]
+
+    def dense(rows, fresh):
+        state = zero[rows, :].astype(f32)
+        a = norm(state, gain[1, 0:1]).astype(bf16)
+        if fresh:
+            ready("up")
+        hidden = [dot(a, up[:, lanes]) for lanes in halves(up)]
+        for lanes, z in zip(halves(up), hidden):
+            value, gradient = gelu_both(z)
+            active[rows, lanes] = value.astype(bf16)
+            slope[rows, lanes] = gradient.astype(bf16)
+        for start, _ in kept:
+            start(fresh)
+        if fresh:
+            ready("down")
+        layer = state + dot(active[rows, :], down[...])
+        one[rows, :] = layer.astype(bf16)
+        exit_part(layer, gain[1, 1:2], cols, rows, False, scores, exit_grad, fresh, sentences)
+
+    leaving = moves.leaving
+    moves.leaving = [kept_wait for _, kept_wait in kept]
+    over(meta, FLAG_T, length, dense)
+    moves.away(one, one_out, FLAG_T)
+    all_of(*leaving)
+    attention(
+        1, one, two, (qkv_out2, o1_out2, l1_2, mid_out2, q2_out2, kv_out2, o2_out2, l2_2), two_out
     )
-    moves.away(o2, o2_out, FLAG_T)
-
-    def finish(rows, _):
-        out[rows, :] = (mid[rows, :] + go(rows) * dot(o2[rows, :], last[...])).astype(bf16)
-
-    over(meta, FLAG_T, length, finish)
-    moves.away(out, final, FLAG_T)
     moves.finish()
 
 
-def attention_backward_kernel(
-    layer, meta, bank, x_in, mem_in, gain, go_rows, info,
-    qkv_in, o1_in, l1, mid_in, q2_in, kv_in, o2_in, l2, dh_in, *rest,
+def backward_kernel(
+    meta, bank, x_in, mem_in, gain, cols, info, dh_in, one_in, zero_in, active_in, slope_in, exit_grad,
+    qkv_in0, o1_in0, l1_0, mid_in0, q2_in0, kv_in0, o2_in0, l2_0,
+    qkv_in2, o1_in2, l1_2, mid_in2, q2_in2, kv_in2, o2_in2, l2_2,
+    dx_out, dmem_out, dw_out0, dw_out1, dw_out2, dgain0, dgain1, dgain2,
+    x, mem, qkv, o1, mid, q2, kv, o2, dh, dx, dmem, dw, wide, third, fourth, pairw, last, up, down, active, slope,
+    dstate, do, dqkv, dk, dv, delta, heads, both_q, both_o, sums, acc, semaphores,
 ):
-    entry = layer == 0
-    if entry:
-        dmem_in, *rest = rest
-    (
-        dx_out, dmem_out, dw_out, dgain,
-        x, mem, qkv, o1, mid, q2, kv, o2, dh, dx, dmem, dw,
-        wide, third, fourth, pairw, last,
-        dstate, do, dqkv, dk, dv, delta, heads, both_q, both_o, sums, acc, semaphores,
-    ) = rest
     length, width = x.shape
-    kind, flag_m, top_m = 4 * layer, FLAG_M + 2 * layer, TOP_M + 2 * layer
     moves = Moves(meta, length, semaphores)
-    section = 2 * layer
-    first_here = [
-        moves.pair(dh_in, dh, FLAG_T), moves.whole(bank.at[section, 7], last), moves.pair(o2_in, o2, FLAG_T),
-        moves.pair(q2_in, q2, FLAG_T), moves.pair(kv_in, kv, flag_m),
-    ]
-    if entry:
-        first_here.append(moves.whole(dmem_in, dmem))
-    second_here = [moves.pair(mem_in, mem, flag_m), moves.pair(mid_in, mid, FLAG_T)]
-    second_here += [moves.whole(bank.at[section, 5 + j], pairw.at[:, j * width : (j + 1) * width]) for j in range(2)]
-    second_here += [moves.whole(bank.at[section, 4], fourth)]
-    third_here = [moves.whole(bank.at[section, 3], third), moves.pair(o1_in, o1, FLAG_T), moves.pair(qkv_in, qkv, FLAG_T)]
-    fourth_here = [moves.whole(bank.at[section, j], wide.at[:, j * width : (j + 1) * width]) for j in range(3)]
-    fourth_here += [moves.pair(x_in, x, FLAG_T)]
-    go = (lambda rows: go_rows[rows, layer : layer + 1])
+    here, sent = {}, {}
+
+    def fetch(name, *waits):
+        here.setdefault(name, []).extend(waits)
+
+    def ready(*names):
+        for name in names:
+            all_of(*here.pop(name))
+
+    def send(j, target, value):
+        if j in sent:
+            sent.pop(j)()
+        dw[j] = value.astype(bf16)
+        sent[j] = moves.whole(dw.at[j], target.at[j])
 
     row_of = lax.broadcasted_iota(i32, (HEADS, width), 0)
     lane_of = lax.broadcasted_iota(i32, (HEADS, width), 1)
-    heads[...] = (lane_of // (width // HEADS) == row_of).astype(bf16)
-    dk[...] = jnp.zeros(dk.shape, f32)
-    dv[...] = jnp.zeros(dv.shape, f32)
-    delta[...] = jnp.zeros(delta.shape, f32)
-    if not entry:
-        dmem[...] = jnp.zeros(dmem.shape, bf16)
-    if entry:
-        dx[...] = jnp.zeros(dx.shape, bf16)
-
-    def weight_grad(targets, flag, left, right):
+
+    def fetch_cross(layer):
+        o2_in, q2_in, kv_in = (o2_in0, q2_in0, kv_in0) if layer == 0 else (o2_in2, q2_in2, kv_in2)
+        fetch("cross", moves.whole(bank.at[2 * layer, 7], last), moves.pair(o2_in, o2, FLAG_T))
+        fetch("cross tiles", moves.pair(q2_in, q2, FLAG_T), moves.pair(kv_in, kv, FLAG_M + 2 * layer))
+
+    def fetch_middle(layer):
+        fetch("memory", *side_by_side(moves, bank, 2 * layer, 5, pairw))
+        fetch("middle", moves.whole(bank.at[2 * layer, 4], fourth))
+        fetch("middle", moves.pair(mid_in0 if layer == 0 else mid_in2, mid, FLAG_T))
+
+    def fetch_self(layer):
+        o1_in, qkv_in = (o1_in0, qkv_in0) if layer == 0 else (o1_in2, qkv_in2)
+        fetch("self", moves.whole(bank.at[2 * layer, 3], third), moves.pair(o1_in, o1, FLAG_T))
+        fetch("self tiles", moves.pair(qkv_in, qkv, FLAG_T))
+
+    def fetch_entry(layer):
+        fetch("entry", *side_by_side(moves, bank, 2 * layer, 0, wide))
+
+    def weight_grad(target, targets, flag, left, right):
         size = len(targets) * width
 
         def part(rows, fresh):
             term = dot_tn(left(rows), right(rows))
-            acc[:, :size] = term if fresh else acc[:, :size] + term
+            for n in range(len(targets)):
+                place = slice(n * width, (n + 1) * width)
+                acc[place] = term[:, place] if fresh else acc[place] + term[:, place]
 
         over(meta, flag, length, part)
         for n, j in enumerate(targets):
-            dw[j] = acc[:, n * width : (n + 1) * width].astype(bf16)
-            moves.away(dw.at[j], dw_out.at[j])
-
-    def begin(grad_of, o, out_weight, target):
-        def dy(rows):
-            return (go(rows) * grad_of(rows)).astype(bf16)
-
-        def part(rows, _):
-            grad = dot_nt(dy(rows), out_weight[...]).astype(bf16)
-            do[rows, :] = grad
-            product = grad.astype(f32) * o[rows, :].astype(f32)
-            high = product.astype(bf16)
-            rest = (product - high.astype(f32)).astype(bf16)
-            delta[:, rows] = dot_nt(heads[...], high) + dot_nt(heads[...], rest)
-            dqkv[rows, :width] = jnp.zeros((rows.size, width), bf16)
-
-        over(meta, FLAG_T, length, part)
-        weight_grad([target], FLAG_T, lambda rows: o[rows, :], dy)
-
-    def top_grad(rows):
-        return dh[rows, :].astype(f32)
-
-    for wait in first_here:
-        wait()
-    begin(top_grad, o2, last, 7)
-    attend_back(
-        meta, CROSS + kind, top_m, info, 2, (q2, 0), (kv, 0), (kv, width), l2, delta, do, (dqkv, 0), dk, dv,
-        both_q, both_o, sums,
-    )
-    for wait in second_here:
-        wait()
-
-    def memory_out(rows, _):
-        dqkv[rows, width : 2 * width] = dk[rows, :].astype(bf16)
-        dqkv[rows, 2 * width :] = dv[rows, :].astype(bf16)
-        term = dot_nt(dqkv[rows, width:], pairw[...])
-        dmem[rows, :] = (dmem[rows, :].astype(f32) + term).astype(bf16)
-
-    over(meta, flag_m, length, memory_out)
-    moves.away(dmem, dmem_out)
-    weight_grad([5, 6], flag_m, lambda rows: mem[rows, :], lambda rows: dqkv[rows, width:])
-
-    def cross_out(rows, fresh):
-        grad_x, grad_gain = norm_back(mid[rows, :], gain[section, 1:2], dot_nt(dqkv[rows, :width], fourth[...]))
-        dstate[rows, :] = top_grad(rows) + grad_x
-        dgain[1:2, :] = grad_gain if fresh else dgain[1:2, :] + grad_gain
-
-    over(meta, FLAG_T, length, cross_out)
-    weight_grad(
-        [4], FLAG_T, lambda rows: norm(mid[rows, :], gain[section, 1:2]).astype(bf16), lambda rows: dqkv[rows, :width]
-    )
-    for wait in third_here:
-        wait()
-    dk[...] = jnp.zeros(dk.shape, f32)
-    dv[...] = jnp.zeros(dv.shape, f32)
-    begin(lambda rows: dstate[rows, :], o1, third, 3)
-    attend_back(
-        meta, SELF + kind, TOP_T, info, 0, (qkv, 0), (qkv, width), (qkv, 2 * width), l1, delta, do, (dqkv, 0), dk, dv,
-        both_q, both_o, sums,
-    )
-    for wait in fourth_here:
-        wait()
-
-    def self_out(rows, fresh):
-        dqkv[rows, width : 2 * width] = dk[rows, :].astype(bf16)
-        dqkv[rows, 2 * width :] = dv[rows, :].astype(bf16)
-        grad_x, grad_gain = norm_back(x[rows, :].astype(f32), gain[section, 0:1], dot_nt(dqkv[rows, :], wide[...]))
-        value = dstate[rows, :] + grad_x
-        if entry:
-            value = jnp.where(go_rows[rows, 2:3] > 0.0, value, 0.0)
-        dx[rows, :] = value.astype(bf16)
-        dgain[0:1, :] = grad_gain if fresh else dgain[0:1, :] + grad_gain
-
-    over(meta, FLAG_T, length, self_out)
-    if entry:
-        moves.away(dx, dx_out)
-    else:
-        moves.away(dx, dx_out, FLAG_T)
-    weight_grad(
-        [0, 1, 2], FLAG_T, lambda rows: norm(x[rows, :].astype(f32), gain[section, 0:1]).astype(bf16),
-        lambda rows: dqkv[rows, :],
-    )
+            send(j, target, acc[n * width : (n + 1) * width])
+
+    def attention(layer, grad_in, grad_out, dw_out, dgain, l1, l2, after):
+        kind, flag_m, top_m = 4 * layer, FLAG_M + 2 * layer, TOP_M + 2 * layer
+        section = 2 * layer
+
+        def go(rows):
+            return cols[rows, layer : layer + 1]
+
+        def clear(rows, _):
+            dk[rows, :] = jnp.zeros((rows.size, width), f32)
+            dv[rows, :] = jnp.zeros((rows.size, width), f32)
+
+        def begin(grad_of, o, out_weight, target):
+            def dy(rows):
+                return (go(rows) * grad_of(rows)).astype(bf16)
+
+            def part(rows, _):
+                grad = dot_nt(dy(rows), out_weight[...]).astype(bf16)
+                do[rows, :] = grad
+                product = grad.astype(f32) * o[rows, :].astype(f32)
+                high = product.astype(bf16)
+                rest = (product - high.astype(f32)).astype(bf16)
+                delta[:, rows] = dot_nt(heads[...], high) + dot_nt(heads[...], rest)
+                dqkv[rows, :width] = jnp.zeros((rows.size, width), bf16)
+
+            over(meta, FLAG_T, length, part)
+            weight_grad(dw_out, [target], FLAG_T, lambda rows: o[rows, :], dy)
+
+        def top_grad(rows):
+            return grad_in[rows, :].astype(f32)
+
+        over(meta, flag_m, length, clear)
+        ready("cross")
+        begin(top_grad, o2, last, 7)
+        ready("cross tiles")
+        attend_back(
+            meta, CROSS + kind, top_m, info, 2, (q2, 0), (kv, 0), (kv, width), l2, delta, do, (dqkv, 0), dk, dv,
+            both_q, both_o, sums,
+        )
+        after("cross")
+        ready("memory")
+
+        def memory_out(rows, _):
+            dqkv[rows, width : 2 * width] = dk[rows, :].astype(bf16)
+            dqkv[rows, 2 * width :] = dv[rows, :].astype(bf16)
+            term = dot_nt(dqkv[rows, width:], pairw[...])
+            dmem[rows, :] = (dmem[rows, :].astype(f32) + term).astype(bf16)
+
+        over(meta, flag_m, length, memory_out)
+        if layer == 0:
+            moves.away(dmem, dmem_out)
+        weight_grad(dw_out, [5, 6], flag_m, lambda rows: mem[rows, :], lambda rows: dqkv[rows, width:])
+        ready("middle")
+
+        def cross_out(rows, fresh):
+            grad_normed = dot_nt(dqkv[rows, :width], fourth[...])
+            grad_x, grad_gain = norm_back(mid[rows, :], gain[section, 1:2], grad_normed)
+            dstate[rows, :] = top_grad(rows) + grad_x
+            dgain[1:2, :] = grad_gain if fresh else dgain[1:2, :] + grad_gain
+
+        over(meta, FLAG_T, length, cross_out)
+        weight_grad(
+            dw_out, [4], FLAG_T, lambda rows: norm(mid[rows, :], gain[section, 1:2]).astype(bf16),
+            lambda rows: dqkv[rows, :width],
+        )
+        after("middle")
+        over(meta, FLAG_T, length, clear)
+        ready("self")
+        begin(lambda rows: dstate[rows, :], o1, third, 3)
+        ready("self tiles")
+        attend_back(
+            meta, SELF + kind, TOP_T, info, 0, (qkv, 0), (qkv, width), (qkv, 2 * width), l1, delta, do, (dqkv, 0),
+            dk, dv, both_q, both_o, sums,
+        )
+        after("self")
+        ready("entry", "x")
+        if layer == 0:
+            grad_out[...] = jnp.zeros(grad_out.shape, bf16)
+
+        def self_out(rows, fresh):
+            dqkv[rows, width : 2 * width] = dk[rows, :].astype(bf16)
+            dqkv[rows, 2 * width :] = dv[rows, :].astype(bf16)
+            grad_normed = dot_nt(dqkv[rows, :], wide[...])
+            grad_x, grad_gain = norm_back(x[rows, :].astype(f32), gain[section, 0:1], grad_normed)
+            value = dstate[rows, :] + grad_x
+            if layer == 0:
+                value = jnp.where(cols[rows, 2:3] > 0.0, value, 0.0)
+            grad_out[rows, :] = value.astype(bf16)
+            dgain[0:1, :] = grad_gain if fresh else dgain[0:1, :] + grad_gain
+
+        over(meta, FLAG_T, length, self_out)
+        if layer == 0:
+            moves.away(grad_out, dx_out)
+        weight_grad(
+            dw_out, [0, 1, 2], FLAG_T, lambda rows: norm(x[rows, :].astype(f32), gain[section, 0:1]).astype(bf16),
+            lambda rows: dqkv[rows, :],
+        )
+        after("end")
+
+    def after_two(stage):
+        if stage == "cross":
+            fetch_cross(0)
+            fetch("down", *stacked(moves, bank, 1, 4, down))
+        if stage == "middle":
+            fetch_middle(0)
+            fetch("slope", moves.pair(slope_in, slope, FLAG_T))
+            fetch("active", moves.pair(active_in, active, FLAG_T))
+        if stage == "self":
+            fetch_self(0)
+            fetch("up", *side_by_side(moves, bank, 1, 0, up))
+        if stage == "end":
+            fetch("x", moves.pair(zero_in, x, FLAG_T))
+            fetch_entry(0)
+
+    fetch("dh", moves.pair(dh_in, dh, FLAG_T))
+    fetch_cross(1)
+    heads[...] = (lane_of // (width // HEADS) == row_of).astype(bf16)
+    delta[...] = jnp.zeros(delta.shape, f32)
+    dmem[...] = jnp.zeros(dmem.shape, bf16)
+    ready("dh")
+    fetch_middle(1)
+    fetch("memory", moves.pair(mem_in, mem, FLAG_M))
+    fetch_self(1)
+    fetch_entry(1)
+    fetch("x", moves.pair(one_in, x, FLAG_T))
+    attention(1, dh, dx, dw_out2, dgain2, l1_2, l2_2, after_two)
+
+    ready("down", "slope")
+
+    def hidden(rows, fresh):
+        for lanes in halves(up):
+            grad = dot_nt(dx[rows, :], down[lanes])
+            slope[rows, lanes] = (slope[rows, lanes].astype(f32) * grad).astype(bf16)
+
+    over(meta, FLAG_T, length, hidden)
+    ready("active")
+
+    def down_part(rows, fresh):
+        term = dot_tn(active[rows, :], dx[rows, :])
+        acc[...] = term if fresh else acc[...] + term
+
+    over(meta, FLAG_T, length, down_part)
+    parts = acc.shape[0] // width
+    for j in range(parts):
+        send(parts + j, dw_out1, acc[j * width : (j + 1) * width])
+    ready("x", "up")
+
+    def normalise(rows, _):
+        do[rows, :] = norm(x[rows, :].astype(f32), gain[1, 0:1]).astype(bf16)
+
+    over(meta, FLAG_T, length, normalise)
+
+    def up_part(rows, fresh):
+        term = dot_tn(do[rows, :], slope[rows, :])
+        for j in range(parts):
+            place = slice(j * width, (j + 1) * width)
+            acc[place] = term[:, place] if fresh else acc[place] + term[:, place]
+
+    over(meta, FLAG_T, length, up_part)
+    for j in range(parts):
+        send(j, dw_out1, acc[j * width : (j + 1) * width])
+
+    def back(rows, fresh):
+        grad_normed = dot_nt(slope[rows, :], up[...])
+        grad_x, grad_gain = norm_back(x[rows, :].astype(f32), gain[1, 0:1], grad_normed)
+        dh[rows, :] = (dx[rows, :].astype(f32) + grad_x).astype(bf16)
+        dgain1[0:1, :] = grad_gain if fresh else dgain1[0:1, :] + grad_gain
+
+    over(meta, FLAG_T, length, back)
+    dgain1[1:2, :] = exit_grad[...]
+    fetch("x", moves.pair(x_in, x, FLAG_T))
+    attention(0, dh, dx, dw_out0, dgain0, l1_0, l2_0, lambda stage: None)
+    all_of(*sent.values())
     moves.finish()
 
 
@@ -458,11 +649,14 @@
     exit_grad[...] = term if fresh else exit_grad[...] + term
 
 
-def dense_weights(moves, bank, section, up, down, width):
+def up_weights(moves, bank, section, up, width):
     parts = up.shape[1] // width
-    here = [moves.whole(bank.at[section, j], up.at[:, j * width : (j + 1) * width]) for j in range(parts)]
-    later = [moves.whole(bank.at[section, parts + j], down.at[j * width : (j + 1) * width]) for j in range(parts)]
-    return here, later
+    return [moves.whole(bank.at[section, j], up.at[:, j * width : (j + 1) * width]) for j in range(parts)]
+
+
+def down_weights(moves, bank, section, down, width):
+    parts = down.shape[0] // width
+    return [moves.whole(bank.at[section, parts + j], down.at[j * width : (j + 1) * width]) for j in range(parts)]
 
 
 def halves(up):
@@ -470,138 +664,86 @@
     return [slice(i * hidden // 2, (i + 1) * hidden // 2) for i in range(2)]
 
 
-def dense_forward_kernel(
-    sentences, meta, bank, x_in, gain, cols, final, active_out, slope_out, scores, exit_grad,
-    x, out, active, slope, up, down, semaphores
-):
-    section = 1
-    length, width = x.shape
-    moves = Moves(meta, length, semaphores)
-    x_here = moves.pair(x_in, x, FLAG_T)
-    here, later = dense_weights(moves, bank, section, up, down, width)
-    x_here()
-
+def dense_gradient(meta, moves, length, acc, left, right, pieces):
     def part(rows, fresh):
-        state = x[rows, :].astype(f32)
-        a = norm(state, gain[section, 0:1]).astype(bf16)
-        if fresh:
-            for wait in here:
-                wait()
-        hidden = [dot(a, up[:, lanes]) for lanes in halves(up)]
-        for lanes, z in zip(halves(up), hidden):
-            value, gradient = gelu_both(z)
-            active[rows, lanes] = value.astype(bf16)
-            slope[rows, lanes] = gradient.astype(bf16)
-        if fresh:
-            for wait in later:
-                wait()
-        layer = state + dot(active[rows, :], down[...])
-        out[rows, :] = layer.astype(bf16)
-        exit_part(layer, gain[section, 1:2], cols, rows, False, scores, exit_grad, fresh, sentences)
+        term = dot_tn(left[rows, :], right[rows, :])
+        rows_, lanes_ = term.shape
+        acc[:rows_, :lanes_] = term if fresh else acc[:rows_, :lanes_] + term
 
     over(meta, FLAG_T, length, part)
-    moves.away(out, final, FLAG_T)
-    moves.away(active, active_out, FLAG_T)
-    moves.away(slope, slope_out, FLAG_T)
-    moves.finish()
-
-
-def dense_gradients(moves, dw, dw_out, grad_up, grad_down, width):
-    parts = grad_up.shape[1] // width
-    for j in range(parts):
-        dw[parts + j] = grad_down[j * width : (j + 1) * width, :].astype(bf16)
-        moves.away(dw.at[parts + j], dw_out.at[parts + j])
-        dw[j] = grad_up[:, j * width : (j + 1) * width].astype(bf16)
-        moves.away(dw.at[j], dw_out.at[j])
-
-
-def accumulate(target, fresh, lanes, value):
-    target[lanes] = value if fresh else target[lanes] + value
+    for block_, place, target in pieces:
+        place[...] = block_().astype(bf16)
+        moves.away(place, target)
+
+
+def down_pieces(acc, dw, dw_out, width):
+    parts = dw.shape[0] // 2
+    return [
+        (lambda j=j: acc[j * width : (j + 1) * width, :], dw.at[parts + j], dw_out.at[parts + j]) for j in range(parts)
+    ]
+
+
+def up_pieces(acc, dw, dw_out, width):
+    return [
+        (lambda j=j: acc[:, j * width : (j + 1) * width], dw.at[j], dw_out.at[j]) for j in range(dw.shape[0] // 2)
+    ]
 
 
 def dense_last_kernel(
     sentences, meta, bank, x_in, gain, cols, dh_in, before, dx_out, dw_out, dgain, states, halt,
-    x, dh, scores, exit_grad, out, dx, dw, active, dhidden, up, down, grad_up, grad_down, semaphores
+    x, dh, dy, normed, scores, exit_grad, out, dx, dw, active, dhidden, up, down, acc_up, acc_down, semaphores
 ):
     section = 3
     length, width = x.shape
     moves = Moves(meta, length, semaphores)
-    x_here, dh_here = moves.pair(x_in, x, FLAG_T), moves.pair(dh_in, dh, FLAG_T)
-    here, later = dense_weights(moves, bank, section, up, down, width)
+    x_here = moves.pair(x_in, x, FLAG_T)
+    up_here = up_weights(moves, bank, section, up, width)
     out[...] = jnp.zeros(out.shape, bf16)
     scores[...] = jnp.zeros(scores.shape, f32)
     x_here()
-    dh_here()
-
-    def part(rows, fresh):
-        go, own = cols[rows, 1:2], cols[rows, 2:3] > 0.0
-        grad_out = jnp.where(own, dh[rows, :].astype(f32), 0.0)
+
+    def forward(rows, fresh):
+        own = cols[rows, 2:3] > 0.0
         state = x[rows, :].astype(f32)
         a = norm(state, gain[section, 0:1]).astype(bf16)
-        dy = (go * grad_out).astype(bf16)
+        normed[rows, :] = a
         if fresh:
-            for wait in here + later:
-                wait()
-        here_rows = slice(0, rows.size)
+            all_of(*up_here)
+            down_here = down_weights(moves, bank, section, down, width) + [moves.pair(dh_in, dh, FLAG_T)]
         hidden = [dot(a, up[:, lanes]) for lanes in halves(up)]
+        if fresh:
+            all_of(*down_here)
+        go = cols[rows, 1:2]
+        dy[rows, :] = (go * jnp.where(own, dh[rows, :].astype(f32), 0.0)).astype(bf16)
         for lanes, z in zip(halves(up), hidden):
-            grad = dot_nt(dy, down[lanes])
+            grad = dot_nt(dy[rows, :], down[lanes])
             value, gradient = gelu_both(z)
-            active[here_rows, lanes] = value.astype(bf16)
-            dhidden[here_rows, lanes] = (gradient * grad).astype(bf16)
-        layer = state + go * dot(active[here_rows, :], down[...])
+            active[rows, lanes] = value.astype(bf16)
+            dhidden[rows, lanes] = (gradient * grad).astype(bf16)
+        layer = state + go * dot(active[rows, :], down[...])
         out[rows, :] = jnp.where(own, layer, 0.0).astype(bf16)
         exit_part(layer, gain[section, 1:2], cols, rows, True, scores, exit_grad, fresh, sentences)
-        grad_x, grad_gain = norm_back(state, gain[section, 0:1], dot_nt(dhidden[here_rows, :], up[...]))
-        dx[rows, :] = (grad_out + grad_x).astype(bf16)
-        dgain[0:1, :] = grad_gain if fresh else dgain[0:1, :] + grad_gain
-        accumulate(grad_down, fresh, slice(None), dot_tn(active[here_rows, :], dy))
-        accumulate(grad_up, fresh, slice(None), dot_tn(a, dhidden[here_rows, :]))
-
-    over(meta, FLAG_T, length, part)
-    moves.away(dx, dx_out, FLAG_T)
+
+    over(meta, FLAG_T, length, forward)
     moves.away(out, states)
+    dense_gradient(meta, moves, length, acc_down, active, dy, down_pieces(acc_down, dw, dw_out, width))
+    dense_gradient(meta, moves, length, acc_up, normed, dhidden, up_pieces(acc_up, dw, dw_out, width))
     dgain[1:2, :] = exit_grad[...]
     lane = lax.broadcasted_iota(i32, (BLOCK, 8), 1)
     for i in range(length // BLOCK):
         rows = slice(i * BLOCK, (i + 1) * BLOCK)
         both = jnp.where(lane == 0, before[rows, :], scores[rows, :])
         halt[:, rows] = jnp.where(cols[rows, 2:3] > 0.0, both, 0.0).T
-    dense_gradients(moves, dw, dw_out, grad_up, grad_down, width)
-    moves.finish()
-
-
-def dense_backward_kernel(
-    meta, bank, x_in, gain, cols, dh_in, active_in, slope_in, exit_grad, dx_out, dw_out, dgain,
-    x, dh, dx, dw, active, slope, dhidden, up, down, grad_up, grad_down, semaphores
-):
-    section = 1
-    length, width = x.shape
-    moves = Moves(meta, length, semaphores)
-    dh_here = moves.pair(dh_in, dh, FLAG_T)
-    later, here = dense_weights(moves, bank, section, up, down, width)
-    here.append(moves.pair(slope_in, slope, FLAG_T))
-    here += [moves.pair(active_in, active, FLAG_T), moves.pair(x_in, x, FLAG_T)]
-    dgain[1:2, :] = exit_grad[...]
-    for wait in [dh_here] + here + later:
-        wait()
-
-    def part(rows, fresh):
-        dy = dh[rows, :]
-        grads = [dot_nt(dy, down[lanes]) for lanes in halves(up)]
-        for lanes, grad in zip(halves(up), grads):
-            dhidden[rows, lanes] = (slope[rows, lanes].astype(f32) * grad).astype(bf16)
-        state = x[rows, :].astype(f32)
-        a = norm(state, gain[section, 0:1]).astype(bf16)
-        grad_x, grad_gain = norm_back(state, gain[section, 0:1], dot_nt(dhidden[rows, :], up[...]))
-        dx[rows, :] = (dy.astype(f32) + grad_x).astype(bf16)
+
+    def back(rows, fresh):
+        grad_out = jnp.where(cols[rows, 2:3] > 0.0, dh[rows, :].astype(f32), 0.0)
+        grad_normed = dot_nt(dhidden[rows, :], up[...])
+        grad_x, grad_gain = norm_back(x[rows, :].astype(f32), gain[section, 0:1], grad_normed)
+        dx[rows, :] = (grad_out + grad_x).astype(bf16)
         dgain[0:1, :] = grad_gain if fresh else dgain[0:1, :] + grad_gain
-        accumulate(grad_down, fresh, slice(None), dot_tn(active[rows, :], dy))
-        accumulate(grad_up, fresh, slice(None), dot_tn(a, dhidden[rows, :]))
-
-    over(meta, FLAG_T, length, part)
+
+    over(meta, FLAG_T, length, back)
     moves.away(dx, dx_out, FLAG_T)
-    dense_gradients(moves, dw, dw_out, grad_up, grad_down, width)
     moves.finish()
 
 
@@ -767,56 +909,69 @@
         out_specs=[spec for spec, _, _ in outs],
         scratch_shapes=[pltpu.VMEM(shape, dtype) for shape, dtype in scratch]
         + [pltpu.SemaphoreType.DMA((semaphores,))],
-        compiler_params=pltpu.CompilerParams(vmem_limit_bytes=60 * 2**20),
+        compiler_params=pltpu.CompilerParams(vmem_limit_bytes=63 * 2**20),
         cost_estimate=pl.CostEstimate(flops=flops, bytes_accessed=20 * 2**20, transcendentals=0),
         name=name,
     )(*args)
 
 
-def attention_forward(layer, plan, bank, x, mem, gain, name):
+def forward(plan, bank, x, mem, gain, sentences):
     meta, info, cols = plan
     length, width = x.shape
     pairs = width // BLOCK
+    hidden = bank.shape[1] // 2 * width
 
     def rows(n, dtype=bf16):
         return ((length, n * width), dtype)
 
+    def put(shape, dtype):
+        return (ANY, shape, dtype)
+
     logs = (VMEM, (HEADS, length), f32)
-    kept = [rows(3), rows(1), logs[1:], rows(1, f32), rows(1), rows(2), rows(1), logs[1:], rows(1)]
-    outs = [(VMEM if shape[0] == HEADS else ANY, shape, dtype) for shape, dtype in kept]
+    inner = ((length, hidden), bf16)
+    saved = [put(*rows(3)), put(*rows(1)), logs, put(*rows(1, f32)), put(*rows(1)), put(*rows(2)), put(*rows(1)), logs,
+             put(*rows(1))]
+    outs = saved + [put(*rows(1)), put(*inner), put(*inner), (VMEM, cols.shape, f32), (VMEM, (1, width), f32)] + saved
     square = ((width, width), bf16)
     scratch = [
-        rows(1), rows(1), rows(3), rows(1), rows(1, f32), rows(1), rows(2), rows(1), rows(1),
+        rows(1), rows(1), rows(3), rows(1), rows(1, f32), rows(1), rows(2), rows(1), rows(1), rows(1), rows(1), inner, inner,
         ((width, 3 * width), bf16), square, square, ((width, 2 * width), bf16), square,
+        ((width, hidden), bf16), ((hidden, width), bf16),
         ((pairs, 2 * BLOCK, BLOCK), bf16), ((8, 2 * BLOCK), f32), ((8, 2 * BLOCK), f32), ((pairs, BLOCK, BLOCK), f32),
     ]
-    return run(
-        functools.partial(attention_forward_kernel, layer), [SMEM, ANY, ANY, ANY, VMEM, VMEM, VMEM], outs, scratch, 32,
-        name, 6 * 10**9, meta, bank, x, mem, gain, cols, info,
+    results = run(
+        functools.partial(forward_kernel, sentences), [SMEM, ANY, ANY, ANY, VMEM, VMEM, VMEM], outs, scratch, 96,
+        "forward", 16 * 10**9, meta, bank, x, mem, gain, cols, info,
     )
-
-
-def attention_backward(layer, plan, bank, x, mem, gain, saved, dh, dmem, name):
+    return results[:8], results[8], results[9:14], results[14:22], results[22]
+
+
+def backward(plan, bank, x, mem, gain, dh, one, zero, active, slope, exit_grad, saved0, saved2):
     meta, info, cols = plan
     length, width = x.shape
     pairs = width // BLOCK
+    hidden = bank.shape[1] // 2 * width
 
     def rows(n, dtype=bf16):
         return ((length, n * width), dtype)
 
     square, matrices = ((width, width), bf16), (bank.shape[1:], bf16)
-    outs = [(ANY, *rows(1)), (ANY, *rows(1)), (ANY, *matrices), (VMEM, (2, width), f32)]
+    gains = [(VMEM, (2, width), f32)] * 3
+    outs = [(ANY, *rows(1)), (ANY, *rows(1))] + [(ANY, *matrices)] * 3 + gains
     both = ((pairs, 2 * BLOCK, BLOCK), bf16)
+    inner = ((length, hidden), bf16)
     scratch = [
         rows(1), rows(1), rows(3), rows(1), rows(1, f32), rows(1), rows(2), rows(1), rows(1), rows(1), rows(1), matrices,
         ((width, 3 * width), bf16), square, square, ((width, 2 * width), bf16), square,
+        ((width, hidden), bf16), ((hidden, width), bf16), inner, inner,
         rows(1, f32), rows(1), rows(3), rows(1, f32), rows(1, f32), ((HEADS, length), f32), ((HEADS, width), bf16),
-        both, both, ((pairs, BLOCK, BLOCK), f32), ((width, 3 * width), f32),
+        both, both, ((pairs, BLOCK, BLOCK), f32), ((hidden, width), f32),
     ]
-    ins = [SMEM, ANY, ANY, ANY, VMEM, VMEM, VMEM, ANY, ANY, VMEM, ANY, ANY, ANY, ANY, VMEM, ANY] + [ANY] * len(dmem)
+    kept = [ANY, ANY, VMEM, ANY, ANY, ANY, ANY, VMEM]
+    ins = [SMEM, ANY, ANY, ANY, VMEM, VMEM, VMEM] + [ANY] * 5 + [VMEM] + kept + kept
     return run(
-        functools.partial(attention_backward_kernel, layer), ins, outs, scratch, 48,
-        name, 12 * 10**9, meta, bank, x, mem, gain, cols, info, *saved, dh, *dmem,
+        backward_kernel, ins, outs, scratch, 160, "backward", 30 * 10**9,
+        meta, bank, x, mem, gain, cols, info, dh, one, zero, active, slope, exit_grad, *saved0, *saved2,
     )
 
 
@@ -824,17 +979,6 @@
     length, width = x.shape
     hidden = bank.shape[1] // 2 * width
     return ((length, width), bf16), ((length, hidden), bf16), ((width, hidden), bf16), ((hidden, width), bf16)
-
-
-def dense_forward(plan, bank, x, gain, sentences, name):
-    meta, _, cols = plan
-    wide, inner, up, down = dense_shapes(bank, x)
-    outs = [(ANY, *wide), (ANY, *inner), (ANY, *inner), (VMEM, cols.shape, f32), (VMEM, (1, x.shape[1]), f32)]
-    return run(
-        functools.partial(dense_forward_kernel, sentences), [SMEM, ANY, ANY, VMEM, VMEM], outs,
-        [wide, wide, inner, inner, up, down], 24,
-        name, 4 * 10**9, meta, bank, x, gain, cols,
-    )
 
 
 def dense_last(plan, bank, x, gain, dh, before, sentences, name):
@@ -843,8 +987,7 @@
     length, width = x.shape
     matrices = (bank.shape[1:], bf16)
     outs = [(ANY, *wide), (ANY, *matrices), (VMEM, (2, width), f32), (ANY, *wide), (VMEM, (8, length), f32)]
-    inner = ((length * 5 // 8, inner[0][1]), bf16)
-    scratch = [wide, wide, (cols.shape, f32), ((1, width), f32), wide, wide, matrices, inner, inner, up, down,
+    scratch = [wide, wide, wide, wide, (cols.shape, f32), ((1, width), f32), wide, wide, matrices, inner, inner, up, down,
                (up[0], f32), (down[0], f32)]
     return run(
         functools.partial(dense_last_kernel, sentences), [SMEM, ANY, ANY, VMEM, VMEM, ANY, VMEM], outs, scratch, 32,
@@ -852,29 +995,13 @@
     )
 
 
-def dense_backward(plan, bank, x, gain, dh, active, slope, exit_grad, name):
-    meta, _, cols = plan
-    wide, inner, up, down = dense_shapes(bank, x)
-    matrices = (bank.shape[1:], bf16)
-    outs = [(ANY, *wide), (ANY, *matrices), (VMEM, (2, x.shape[1]), f32)]
-    scratch = [wide, wide, wide, matrices, inner, inner, inner, up, down, (up[0], f32), (down[0], f32)]
-    return run(
-        dense_backward_kernel, [SMEM, ANY, ANY, VMEM, VMEM, ANY, ANY, ANY, VMEM], outs, scratch, 32,
-        name, 8 * 10**9, meta, bank, x, gain, cols, dh, active, slope, exit_grad,
-    )
-
-
 def row_forward_backward(row, core, x, mem, cotangent, bank, gains, ints):
     plan = make_plan(row, core, ints)
     sentences = ints[-1].shape[-1]
-    *saved0, zero = attention_forward(0, plan, bank, x, mem, gains, "attend_zero")
-    one, active, slope, scores, exit0 = dense_forward(plan, bank, zero, gains, sentences, "dense_one")
-    *saved2, two = attention_forward(1, plan, bank, one, mem, gains, "attend_two")
+    saved0, zero, (one, active, slope, scores, exit0), saved2, two = forward(plan, bank, x, mem, gains, sentences)
     dtwo, dw3, dgain3, states, halt = dense_last(plan, bank, two, gains, cotangent, scores, sentences, "dense_three")
-    done, dmem, dw2, dgain2 = attention_backward(1, plan, bank, one, mem, gains, saved2, dtwo, (), "attend_two_back")
-    dzero, dw1, dgain1 = dense_backward(plan, bank, zero, gains, done, active, slope, exit0, "dense_one_back")
-    dx, dmem, dw0, dgain0 = attention_backward(
-        0, plan, bank, x, mem, gains, saved0, dzero, (dmem,), "attend_zero_back"
+    dx, dmem, dw0, dw1, dw2, dgain0, dgain1, dgain2 = backward(
+        plan, bank, x, mem, gains, dtwo, one, zero, active, slope, exit0, saved0, saved2
     )
     return states, halt, dx, dmem, [dw0, dw1, dw2, dw3], [dgain0, dgain1, dgain2, dgain3]
 

time: 362 us -> 335 us (0.925)
  Pallas kernels: 353 us -> 328 us
    pallas_call x7 -> x3, Pallas kernels: 134 us -> 105 us  [run(): pl.pallas_call(kernel, out_shape=[jax.ShapeDtypeStruct(shape, dtype) for...]
    pallas_call x1, Pallas kernels: 132 us -> 136 us  [reduce_all(): pl.pallas_call(reduce_kernel, out_shape=outs, in_specs=[ANY] * 4 + [VMEM]...]
where the time goes in v3:
time: 335 us; the launch traced here: 330 us
  Pallas kernels  328 us (98%)
    pallas_call x1, Pallas kernels, reduce_all(): pl.pallas_call(reduce_kernel, out_shape=outs, in_specs=[ANY] * 4 + [VMEM]...  136 us
    pallas_call x3, Pallas kernels, run(): pl.pallas_call(kernel, out_shape=[jax.ShapeDtypeStruct(shape, dtype) for...  105 us
    pallas_call x1, Pallas kernels, gather_all(): pl.pallas_call(gather_kernel, out_shape=outs, in_specs=[ANY] * 10, out_sp...  76.3 us
    pallas_call x1, Pallas kernels, widen(): pl.pallas_call(widen_kernel, grid=(steps,), out_shape=[jax.ShapeDtypeStru...  7.85 us

profile of v3, /device:TPU:0, one launch (start us, length us, event | category | flops | bytes accessed | tf_op | source)
XLA Modules:
  0.0 330.4 jit_solution(8255103647698008594)
XLA Ops:
  0.6 76.3 %gather_all.1 = (bf16[1024,512]{1,0:T(8,128)(2,1)}, bf16[1024,512]{1,0:T(8,128)(2,1)}, bf16[1024,512]{1,0:T(8,128)(2,1)}, bf16[16384,512]{1,0:T(8,128)(2,1)}, f3...) custom-call(bf16[2,1024,128]{2,1,0:T(8,128)(2,1)} %states.1, ...), custom_call_target="tpu_custom_call" | custom-call | tf_op jit(solution)/shard_map/gather_all/pallas_call | solution.py:1189
  76.9 2.5 make_plan.1
  79.5 33.4 %forward.1 = (bf16[1024,1536]{1,0:T(8,128)(2,1)}, bf16[1024,512]{1,0:T(8,128)(2,1)}, f32[8,1024]{1,0:T(8,128)}, f32[1024,512]{1,0:T(8,128)}, bf16[1024,512]{1,0:...) custom-call(s32[8,128]{1,0:T(8,128)} %get-tuple-element.70.meta, ...), custom_call_target="tpu_custom_call" | custom-call | flops 16000000000 | bytes 20971520 | tf_op jit(solution)/shard_map/forward/pallas_call | solution.py:905
  112.9 18.5 %dense_three.1 = (bf16[1024,512]{1,0:T(8,128)(2,1)}, bf16[8,512,512]{2,1,0:T(8,128)(2,1)}, f32[2,512]{1,0:T(2,128)}, bf16[1024,512]{1,0:T(8,128)(2,1)}, f32[8,1024]{1,0:T(8,128)}) custom-call(s32[8,128]{1,0:T(8,128)} %get-tuple-element.70.meta, bf16[4,8,512,512]{3,2,1,0:T(8,128)(2,1)} %bitcast.19, bf16[1024,512]{1,0:T(8,128)(2,1)} %get-tuple-element.77.x_in, ...), custom_call_target="tpu_custom_call" | custom-call | flops 8000000000 | bytes 20971520 | tf_op jit(solution)/shard_map/dense_three/pallas_call | solution.py:905
  131.4 53.2 %backward.1 = (bf16[1024,512]{1,0:T(8,128)(2,1)}, bf16[1024,512]{1,0:T(8,128)(2,1)}, bf16[8,512,512]{2,1,0:T(8,128)(2,1)}, bf16[8,512,512]{2,1,0:T(8,128)(2,1)},...) custom-call(s32[8,128]{1,0:T(8,128)} %get-tuple-element.70.meta, ...), custom_call_target="tpu_custom_call" | custom-call | flops 30000001024 | bytes 20971520 | tf_op jit(solution)/shard_map/backward/pallas_call | solution.py:905
  184.6 136.3 %reduce_all.1 = (bf16[4096,512]{1,0:T(8,128)(2,1)}, f32[2,512]{1,0:T(2,128)}, bf16[2,1024,128]{2,1,0:T(8,128)(2,1)}, bf16[2,1024,128]{2,1,0:T(8,128)(2,1)}, bf16...) custom-call(bf16[4096,512]{1,0:T(8,128)(2,1)} %bitcast.13, bf16[4096,512]{1,0:T(8,128)(2,1)} %bitcast.14, ...), custom_call_target="tpu_custom_call" | custom-call | tf_op jit(solution)/shard_map/reduce_all/pallas_call | solution.py:1560
  320.9 0.0 copy-start
  320.9 0.0 copy-start.1
  321.0 7.8 %widen.1 = (f32[4096,512]{1,0:T(8,128)}, f32[2,1024,128]{2,1,0:T(8,128)}, f32[2,1024,128]{2,1,0:T(8,128)}, f32[2,2,256]{2,1,0:T(2,128)}) custom-call(bf16[4096,512]{1,0:T(8,128)(2,1)} %get-tuple-element.115.bank, bf16[2,1024,128]{2,1,0:T(8,128)(2,1)} %get-tuple-element.116.dx, bf16[2,1024,128]{2,1,0:T(8,128)(2,1)} %get-tuple-element.117.dmem, ...), custom_call_target="tpu_custom_call" | custom-call | tf_op jit(solution)/shard_map/widen/pallas_call | solution.py:768
  328.8 0.0 copy-done
  328.8 0.8 copy.18
  329.6 0.0 copy-done.1
  329.6 0.6 copy.19
Async XLA Ops:
  320.9 7.9 %copy-start = (bf16[2,1024,128]{2,1,0:T(8,128)(2,1)S(1)}, bf16[2,1024,128]{2,1,0:T(8,128)(2,1)}, u32[]{:S(2)}) copy-start(bf16[2,1024,128]{2,1,0:T(8,128)(2,1)} %get-tuple-element.130) | copy-start | bytes 1572868
  320.9 8.7 %copy-start.1 = (f32[2,512]{1,0:T(2,128)S(1)}, f32[2,512]{1,0:T(2,128)}, u32[]{:S(2)}) copy-start(f32[2,512]{1,0:T(2,128)} %get-tuple-element.123) | copy-start | bytes 12292
